TPU v7x, 256 devices: a whole 4x4x8 slice. The times are simulated.
256 devices in a mesh: tm: 16 (over y, x_hi, core), space: 16 (over z, x_lo).
Axes of the slice: x: 4 (x_hi: 2, x_lo: 2; x = x_hi * 2 + x_lo), y: 4, z: 8, core: 2. Of those that a mesh axis runs over, the one named last changes fastest.
Arguments:
- frames: bfloat16 [128, 16, 16, 2048], P('tm', 'space'), may hold values from -24 to 24
- actions: int32 [128], P('tm'), may hold values from 0 to 7
- action_table: bfloat16 [8, 2048], replicated, may hold values from -5 to 5
- norm_gain: float32 [2048], replicated, may hold values from 0.1 to 1.9
- w_q: bfloat16 [2048, 2048], P(None, 'space'), may hold values from -0.125 to 0.125
- w_kv: bfloat16 [2048, 2, 128], P(None, None, 'space'), may hold values from -0.125 to 0.125
- qk_gain: float32 [2, 128], replicated, may hold values from 0.5 to 10
- w_o: bfloat16 [2048, 2048], P('space'), may hold values from -0.5 to 0.5
- w_up: bfloat16 [2048, 8192], P(None, 'space'), may hold values from -0.125 to 0.125
- w_down: bfloat16 [8192, 2048], P('space'), may hold values from -0.0625 to 0.0625
- w_lat: bfloat16 [2048, 512], replicated, may hold values from -0.125 to 0.125
- w_conv: bfloat16 [3, 3, 512, 512], replicated, may hold values from -0.1875 to 0.1875
- conv_bias: float32 [512], replicated, may hold values from -3 to 3
Outputs:
- decoded: bfloat16 [128, 32, 32, 512], P('tm', 'space')
All inputs are finite; a program needn't handle non-finite values.
Results may differ from a plain program's by a relative error of at most 0.025.
The roundings to bfloat16 on the way count: a program that leaves them out, or rounds other values in their place, can miss the bound.
Values may be sent and summed in bfloat16 or wider, within the bound.
A program may use at most 192 MiB of HBM per device.

v0:
```python
import math

import jax
import jax.numpy as jnp
from jax import lax
from jax.sharding import PartitionSpec as P

epsilon = 1e-06
masked_score = -1e30


def from_behind(value, axis, steps):
    count = lax.axis_size(axis)
    first, last = (max(0, -steps), min(count, count - steps))
    return lax.ppermute(value, axis, [(source, source + steps) for source in range(first, last)])


def root_scale(values, gain):
    return values * lax.rsqrt(jnp.mean(values * values, axis=-1, keepdims=True) + epsilon) * gain


def per_device(
    frames,
    actions,
    action_table,
    norm_gain,
    w_q,
    w_kv,
    qk_gain,
    w_o,
    w_up,
    w_down,
    w_lat,
    w_conv,
    conv_bias,
):
    frame_count, own_rows, grid_width, model_width = frames.shape
    head_size = qk_gain.shape[1]
    space_count = lax.axis_size("space")
    channels = w_lat.shape[1]
    onehot = (
        actions[:, None] == jnp.arange(action_table.shape[0], dtype=jnp.int32)[None, :]
    ).astype(jnp.bfloat16)
    embedding = jnp.dot(onehot, action_table, preferred_element_type=jnp.float32)
    stream = (frames.astype(jnp.float32) + embedding[:, None, None, :]).astype(jnp.bfloat16)
    everyone = lax.all_gather(stream, "space", axis=1, tiled=True)
    normed = root_scale(everyone.astype(jnp.float32), norm_gain).astype(jnp.bfloat16)
    queries = jnp.einsum("fhwd,dk->fhwk", normed, w_q, preferred_element_type=jnp.float32).astype(
        jnp.bfloat16
    )
    pair_cols = jnp.einsum(
        "fhwd,dk->fhwk", normed, w_kv.reshape(model_width, -1), preferred_element_type=jnp.float32
    ).astype(jnp.bfloat16)
    hidden = jax.nn.gelu(
        jnp.einsum("fhwd,dk->fhwk", normed, w_up, preferred_element_type=jnp.float32),
        approximate=True,
    ).astype(jnp.bfloat16)
    query_own, pair_own = (
        lax.all_to_all(queries, "space", split_axis=1, concat_axis=3, tiled=True),
        lax.all_to_all(pair_cols, "space", split_axis=1, concat_axis=3, tiled=True),
    )
    positions = own_rows * grid_width
    head_count = query_own.shape[3] // head_size
    query_heads = root_scale(
        query_own.reshape(frame_count, positions, head_count, head_size).astype(jnp.float32),
        qk_gain[0],
    ).astype(jnp.bfloat16)
    pair_split = pair_own.reshape(frame_count, positions, space_count, 2, head_size // space_count)
    key_rows = root_scale(
        pair_split[:, :, :, 0, :].reshape(frame_count, positions, head_size).astype(jnp.float32),
        qk_gain[1],
    ).astype(jnp.bfloat16)
    value_rows = pair_split[:, :, :, 1, :].reshape(frame_count, positions, head_size)
    key_value = jnp.stack([key_rows, value_rows], axis=2)
    score_scale = 1.0 / math.sqrt(head_size)
    first_frame = lax.axis_index("tm") * frame_count
    query_frames = first_frame + jnp.arange(frame_count, dtype=jnp.int32)

    def absorb(online, pair_piece, start_frame):
        key_frames = start_frame + jnp.arange(pair_piece.shape[0], dtype=jnp.int32)
        allowed = (query_frames[:, None] >= key_frames[None, :])[:, None, None, :]

        def attend(current):
            running_max, totals, weighted = current
            scores = (
                jnp.einsum(
                    "tphd,spd->tphs",
                    query_heads,
                    pair_piece[:, :, 0, :],
                    preferred_element_type=jnp.float32,
                )
                * score_scale
            )
            scores = jnp.where(allowed, scores, masked_score)
            new_max = jnp.maximum(running_max, jnp.max(scores, axis=-1))
            exponent = jnp.where(allowed, jnp.exp(scores - new_max[..., None]), 0.0)
            factor = jnp.exp(running_max - new_max)
            totals = totals * factor + jnp.sum(exponent, axis=-1)
            weighted = weighted * factor[..., None] + jnp.einsum(
                "tphs,spd->tphd",
                exponent.astype(jnp.bfloat16),
                pair_piece[:, :, 1, :],
                preferred_element_type=jnp.float32,
            )
            return (new_max, totals, weighted)

        useful = jnp.logical_and(start_frame >= 0, start_frame <= query_frames[-1])
        return lax.cond(useful, attend, lambda current: current, online)

    start_state = (
        jnp.full((frame_count, positions, head_count), masked_score, jnp.float32),
        jnp.zeros((frame_count, positions, head_count), jnp.float32),
        jnp.zeros((frame_count, positions, head_count, head_size), jnp.float32),
    )
    online = absorb(start_state, key_value, first_frame)

    def advance(hop_index, carried):
        held_block, current = carried
        held_block = from_behind(held_block, "tm", 1)
        return (held_block, absorb(current, held_block, first_frame - hop_index * frame_count))

    online = lax.fori_loop(1, lax.axis_size("tm"), advance, (key_value, online))[1]
    running_max, totals, weighted = online
    attended_own = (
        (weighted / totals[..., None])
        .astype(jnp.bfloat16)
        .reshape(frame_count, own_rows, grid_width, head_count * head_size)
    )
    mixed_heads = lax.all_to_all(attended_own, "space", split_axis=3, concat_axis=1, tiled=True)
    own_stream = jnp.transpose(stream, (1, 0, 2, 3))
    attention_part = jnp.einsum(
        "fhwk,kd->hfwd", mixed_heads, w_o, preferred_element_type=jnp.float32
    )
    row_sums = lax.psum_scatter(
        (
            attention_part
            + jnp.einsum("fhwk,kd->hfwd", hidden, w_down, preferred_element_type=jnp.float32)
        ).astype(jnp.bfloat16),
        "space",
        scatter_dimension=0,
        tiled=True,
    ).astype(jnp.float32)
    block_out = (own_stream.astype(jnp.float32) + row_sums).astype(jnp.bfloat16)
    latent_rows = jax.nn.silu(
        jnp.einsum("hfwd,dc->hfwc", block_out, w_lat, preferred_element_type=jnp.float32)
    ).astype(jnp.bfloat16)
    below_row = from_behind(latent_rows, "space", -1)
    extended = jnp.concatenate([latent_rows, below_row], axis=0)
    zero_column = jnp.zeros((own_rows + 1, frame_count, 1, channels), jnp.bfloat16)
    widened = jnp.concatenate([extended, zero_column], axis=2)
    center = widened[:-1, :, :-1]
    right_cells = widened[:-1, :, 1:]
    below_cells = widened[1:, :, :-1]
    corner = widened[1:, :, 1:]

    def apply_taps(cell_list, tap_list):
        stacked_cells = jnp.concatenate(cell_list, axis=-1)
        stacked_kernel = jnp.concatenate(
            [w_conv[row_tap, col_tap] for row_tap, col_tap in tap_list], axis=0
        )
        return (
            jnp.einsum(
                "hfwc,co->hfwo", stacked_cells, stacked_kernel, preferred_element_type=jnp.float32
            )
            + conv_bias
        )

    even_even = apply_taps([center], [(1, 1)])
    even_odd = apply_taps([right_cells, center], [(1, 0), (1, 2)])
    odd_even = apply_taps([below_cells, center], [(0, 1), (2, 1)])
    odd_odd = apply_taps(
        [corner, below_cells, right_cells, center], [(0, 0), (0, 2), (2, 0), (2, 2)]
    )
    upper = jnp.stack([even_even, even_odd], axis=3)
    lower = jnp.stack([odd_even, odd_odd], axis=3)
    pixel_grid = jnp.stack([upper, lower], axis=1)
    pixel_grid = jnp.transpose(pixel_grid, (2, 0, 1, 3, 4, 5)).reshape(
        frame_count, 2 * own_rows, 2 * grid_width, channels
    )
    return pixel_grid.astype(jnp.bfloat16)


def solution(mesh):
    return jax.shard_map(
        per_device,
        mesh=mesh,
        in_specs=(
            P("tm", "space", None, None),
            P("tm"),
            P(),
            P(),
            P(None, "space"),
            P(None, None, "space"),
            P(),
            P("space", None),
            P(None, "space"),
            P("space", None),
            P(),
            P(),
            P(),
        ),
        out_specs=P("tm", "space", None, None),
        check_vma=False,
    )
```

profile of v0, /device:TPU:18, one launch (start us, length us, event | category | flops | bytes accessed | tf_op | source)
XLA Modules:
  0.0 905.1 jit_solution(997056860177246829)
XLA Ops:
  7.7 2.0 add_convert_fusion.1
  11.7 182.5 %all-gather.2.cloned.1.call-done = bf16[8,16,16,2048]{3,2,0,1:T(8,128)(2,1)} async-done(((bf16[8,1,16,2048]{3,2,0,1:T(8,128)(2,1)}), bf16[8,16,16,2048]{3,2,0,1:T(8,128)(2,1)}) %all-gather.2.cloned.1.call-update) | async-done | bytes 8388624 | tf_op jit(solution)/shard_map/all_gather | solution.py:46
  194.2 5.2 fusion.26
  200.0 2.7 fusion.66
  203.9 8.5 all-to-all-start
  212.4 5.8 fusion.69
  220.1 7.1 all-to-all-start.1
  238.8 3.6 all-to-all-done.1
  244.2 2.2 copy.86
  246.4 9.2 %conditional.2 = (f32[8,16,16]{2,0,1:T(8,128)}, f32[8,16,16]{2,0,1:T(8,128)S(1)}, f32[8,16,16,128]{3,2,0,1:T(8,128)S(1)}) conditional(s32[]{:T(128)} %convert_element_type.139, () %tuple.34, (s32[]{:T(128)}, s32[8,1]{0,1:T(1,128)S(1)}, s32[1,8]{1,0:T(1,128)S(1)}, bf16[8,16,128]{1,2,0:T(8,128)(2,1)}, bf16[8,16,16,128]{3,1,0,2:T(8,128)(2,1)}, ...), branch_computations={%region_3.0_spmd, %region_4.7_spmd} | conditional | flops 8806480 | bytes 2122208 | solution.py:108
  247.5 3.2 fusion.130
  255.6 184.0 %while.19 = (s32[]{:T(128)}, bf16[8,16,2,128]{3,0,1,2:T(8,128)(2,1)}, f32[8,16,16]{2,0,1:T(8,128)}, f32[8,16,16]{2,0,1:T(8,128)S(1)}, f32[8,16,16,128]{3,2,0,1:T...) while((s32[]{:T(128)}, ...), condition=%wide.region_12.13_spmd, body=%wide.region_7.12_spmd.sunk | while | flops 9064528 | bytes 3983979 | solution.py:122
  255.6 1.9 collective-permute-start
  258.9 4.9 collective-permute-done
  263.8 6.0 conditional.4
  263.9 2.4 fusion.131
  270.5 1.9 collective-permute-start
  273.7 4.9 collective-permute-done
  278.7 6.0 conditional.4
  278.8 2.4 fusion.131
  285.3 1.9 collective-permute-start
  288.6 4.9 collective-permute-done
  293.5 6.1 conditional.4
  293.6 2.4 fusion.131
  300.2 1.9 collective-permute-start
  303.4 4.9 collective-permute-done
  308.4 6.0 conditional.4
  308.5 2.4 fusion.131
  315.1 1.9 collective-permute-start
  318.3 4.9 collective-permute-done
  323.2 6.1 conditional.4
  323.3 2.4 fusion.131
  329.9 1.9 collective-permute-start
  333.2 4.9 collective-permute-done
  338.1 6.1 conditional.4
  338.2 2.4 fusion.131
  348.0 4.9 collective-permute-done
  353.0 6.0 conditional.4
  353.1 2.4 fusion.131
  362.9 4.9 collective-permute-done
  367.8 6.1 conditional.4
  367.9 2.4 fusion.131
  377.8 4.9 collective-permute-done
  383.3 3.1 collective-permute-start
  387.8 3.7 collective-permute-done
  395.4 4.9 collective-permute-done
  400.9 4.2 collective-permute-start
  406.5 2.7 collective-permute-done
  409.7 4.2 collective-permute-start
  415.3 2.7 collective-permute-done
  418.6 10.2 %collective-permute-start = (bf16[8,16,2,128]{3,0,1,2:T(8,128)(2,1)}, bf16[8,16,2,128]{3,0,1,2:T(8,128)(2,1)S(1)}, u32[]{:S(2)}, u32[]{:S(2)}) collective-permute-start(bf16[8,16,2,128]{3,0,1,2:T(8,128)(2,1)} %get-tuple-element.401), channel_id=1, source_target_pairs={{0,16},{16,32},{32,48},{48,64},{64,80},{80,96},{96,112},{112,128},... | collective-permute-start | bytes 196616 | tf_op jit(solution)/shard_map/while/body/eval_jaxpr/ppermute | solution.py:15
  430.8 6.8 collective-permute-start
  440.7 4.9 copy.87
  445.6 6.4 reshape.220
  452.0 5.1 all-to-all-start.2
  457.4 15.8 %fusion.44 = f32[8,16,16,2048]{3,2,1,0:T(8,128)} fusion(bf16[512,2048]{1,0:T(8,128)(2,1)S(1)} %copy-done, bf16[2048,512]{1,0:T(8,128)(2,1)} %param.27, bf16[8,16,16,2048]{3,2,0,1:T(8,128)(2,1)} %all-gather.2.cloned.1.call-done, f32[2048]{0:T(1024)S(1)} %copy-done.14, f32[8,16,16]{2,0,1:T(8,128)S(1)} %copy-done.10), kind=kOutput, calls=%fused_computation.61 | convolution fusion | flops 8616148992 | bytes 29376512 | tf_op jit(solution)/shard_map/fhwk,kd->hfwd/dot_general | solution.py:137
  473.2 4.1 reshape.221
  477.3 4.4 copy.89
  481.8 11.4 %fusion.29 = bf16[16,8,16,2048]{3,2,0,1:T(8,128)(2,1)} fusion(f32[8,16,16,2048]{3,2,1,0:T(8,128)} %fusion.44, bf16[128,2048]{1,0:T(8,128)(2,1)S(1)} %copy-done.5, bf16[8,1,16,16,128]{4,2,3,0,1:T(8,128)(2,1)S(1)} %copy.89), kind=kOutput, calls=%fused_computation.45 | convolution fusion | flops 1082130432 | bytes 26214400 | tf_op jit(solution)/shard_map/fhwk,kd->hfwd/dot_general | solution.py:131
  494.4 3.6 slice_bitcast_fusion.7
  498.0 386.7 %all-reduce.4.cloned.1.call-done = bf16[16,8,16,2048]{3,2,0,1:T(8,128)(2,1)} async-done(((bf16[16,8,16,2048]{3,2,0,1:T(8,128)(2,1)}), bf16[16,8,16,2048]{3,2,0,1:T(8,128)(2,1)}) %all-reduce.4.cloned.1.call-update) | async-done | bytes 8388624
  884.6 3.0 multiply_convert_fusion
  887.6 3.4 collective-permute-start.1
  892.4 3.3 collective-permute-done.1
  (204 shorter events, 87.8 us)
Async XLA Ops:
  6.5 450.9 %copy-start = (bf16[512,2048]{1,0:T(8,128)(2,1)S(1)}, bf16[512,2048]{1,0:T(8,128)(2,1)}, u32[]{:S(2)}) copy-start(bf16[512,2048]{1,0:T(8,128)(2,1)} %param.28) | copy-start | bytes 6291460
  6.5 187.7 %all-gather.2.cloned.1.call-start = ((), (), s32[]{:S(2)}) async-start(), calls=%async_computation.3 | async-start | bytes 8912896 | tf_op jit(solution)/shard_map/all_gather | solution.py:46
  9.7 189.8 %copy-start.12 = (bf16[2048,2,8]{0,2,1:T(8,128)(2,1)S(1)}, bf16[2048,2,8]{0,2,1:T(8,128)(2,1)}, u32[]{:S(2)}) copy-start(bf16[2048,2,8]{0,2,1:T(8,128)(2,1)} %param.24) | copy-start | bytes 196612
  9.7 189.8 %copy-start.13 = (f32[2048]{0:T(1024)S(1)}, f32[2048]{0:T(1024)}, u32[]{:S(2)}) copy-start(f32[2048]{0:T(1024)} %param.22) | copy-start | bytes 24580
  194.2 5.8 copy-start.2
  200.0 12.4 %copy-start.9 = (f32[8,16,16]{2,0,1:T(8,128)}, f32[8,16,16]{2,0,1:T(8,128)S(1)}, u32[]{:S(2)}) copy-start(f32[8,16,16]{2,0,1:T(8,128)S(1)} %add_rsqrt_fusion.1) | copy-start | bytes 24580
  200.0 12.4 %copy-start.11 = (bf16[2048,128]{1,0:T(8,128)(2,1)S(1)}, bf16[2048,128]{1,0:T(8,128)(2,1)}, u32[]{:S(2)}) copy-start(bf16[2048,128]{1,0:T(8,128)(2,1)} %param.23) | copy-start | bytes 1572868
  203.9 16.3 %all-to-all-start = ((bf16[16,2,1024]{2,1,0:T(2,128)(2,1)}), bf16[16,2,1024]{2,1,0:T(2,128)(2,1)S(1)}, u32[]{:S(2)}, u32[]{:S(2)}) async-start(bf16[16,2,1024]{2,1,0:T(2,128)(2,1)} %reshape.218), calls=%async_computation | async-start | bytes 131072 | tf_op jit(solution)/shard_map/all_to_all | solution.py:60
  220.1 22.3 %all-to-all-start.1 = ((bf16[8,16,16,128]{3,2,0,1:T(8,128)(2,1)}), bf16[8,16,16,128]{3,2,0,1:T(8,128)(2,1)S(1)}, u32[]{:S(2)}, u32[]{:S(2)}) async-start(bf16[8,16,16,128]{3,2,0,1:T(8,128)(2,1)} %copy.79), calls=%async_computation.1 | async-start | bytes 1048576 | tf_op jit(solution)/shard_map/all_to_all | solution.py:59
  230.0 1.0 copy-start.3
  255.6 8.2 collective-permute-start
  270.5 8.2 collective-permute-start
  285.3 8.2 collective-permute-start
  300.2 8.2 collective-permute-start
  315.1 8.2 collective-permute-start
  329.9 8.2 collective-permute-start
  344.8 8.2 collective-permute-start
  359.6 8.2 collective-permute-start
  374.5 8.2 collective-permute-start
  383.3 8.2 collective-permute-start
  392.1 8.2 collective-permute-start
  400.9 8.2 collective-permute-start
  409.7 8.2 collective-permute-start
  418.6 11.6 %collective-permute-start = (bf16[8,16,2,128]{3,0,1,2:T(8,128)(2,1)}, bf16[8,16,2,128]{3,0,1,2:T(8,128)(2,1)S(1)}, u32[]{:S(2)}, u32[]{:S(2)}) collective-permute-start(bf16[8,16,2,128]{3,0,1,2:T(8,128)(2,1)} %get-tuple-element.401), channel_id=1, source_target_pairs={{0,16},{16,32},{32,48},{48,64},{64,80},{80,96},{96,112},{112,128},... | collective-permute-start | bytes 196616 | tf_op jit(solution)/shard_map/while/body/eval_jaxpr/ppermute | solution.py:15
  430.8 8.2 collective-permute-start
  440.7 16.7 %copy-start.10 = (f32[8,16,16]{2,0,1:T(8,128)S(1)}, f32[8,16,16]{2,0,1:T(8,128)}, u32[]{:S(2)}) copy-start(f32[8,16,16]{2,0,1:T(8,128)} %copy-done.9) | copy-start | bytes 24580
  440.7 16.7 %copy-start.14 = (f32[2048]{0:T(1024)S(1)}, f32[2048]{0:T(1024)}, u32[]{:S(2)}) copy-start(f32[2048]{0:T(1024)} %param.22) | copy-start | bytes 24580
  452.0 21.2 %all-to-all-start.2 = ((bf16[16,2,8192]{2,1,0:T(2,128)(2,1)}), bf16[16,2,8192]{2,1,0:T(2,128)(2,1)S(1)}, u32[]{:S(2)}, u32[]{:S(2)}) async-start(bf16[16,2,8192]{2,1,0:T(2,128)(2,1)} %reshape.220), calls=%async_computation.2 | async-start | bytes 1048576 | tf_op jit(solution)/shard_map/all_to_all | solution.py:129
  457.1 427.5 %all-reduce.4.cloned.1.call-start = ((), (), s32[]{:S(2)}) async-start(), calls=%async_computation.4 | async-start | bytes 16777216
  473.2 8.6 copy-start.5
  493.1 0.7 copy-start.16
  493.2 391.5 %copy-start.4 = (bf16[8,1,16,2048]{3,2,0,1:T(8,128)(2,1)S(1)}, bf16[8,1,16,2048]{3,2,0,1:T(8,128)(2,1)}, u32[]{:S(2)}) copy-start(bf16[8,1,16,2048]{3,2,0,1:T(8,128)(2,1)} %add_convert_fusion.1) | copy-start | bytes 1572868
  494.4 396.7 %copy-start.15 = (f32[512]{0:T(512)S(1)}, f32[512]{0:T(512)}, u32[]{:S(2)}) copy-start(f32[512]{0:T(512)} %param.31) | copy-start | bytes 6148
  884.6 11.2 %copy-start.8 = (bf16[512,512]{1,0:T(8,128)(2,1)S(1)}, bf16[512,512]{1,0:T(8,128)(2,1)}, u32[]{:S(2)}) copy-start(bf16[512,512]{1,0:T(8,128)(2,1)} %get-tuple-element.311) | copy-start | bytes 1572868
  884.6 11.8 %copy-start.6 = (bf16[512,512]{1,0:T(8,128)(2,1)S(1)}, bf16[512,512]{1,0:T(8,128)(2,1)}, u32[]{:S(2)}) copy-start(bf16[512,512]{1,0:T(8,128)(2,1)} %get-tuple-element.312) | copy-start | bytes 1572868
  884.6 11.8 %copy-start.7 = (bf16[512,512]{1,0:T(8,128)(2,1)S(1)}, bf16[512,512]{1,0:T(8,128)(2,1)}, u32[]{:S(2)}) copy-start(bf16[512,512]{1,0:T(8,128)(2,1)} %get-tuple-element.313) | copy-start | bytes 1572868
  887.6 8.0 collective-permute-start.1
  896.4 1.8 copy-start.1
Sparse Core Ops, SparseCore 0:
  9.8 184.3 all-gather.1
  493.3 391.2 all-reduce.3
where the time goes:
time: 911 us; the launch traced here: 905 us
  waiting for transfers between devices  636 us (70%)
  matrix products  73.6 us (8%)
  starting transfers between devices  71.9 us (8%)
  local copies, waits for them, and re-layouts  65.6 us (7%)
  other arithmetic  33.2 us (4%)
  between operations  14.4 us (2%)
  loops' own time  10.8 us (1%)
    unnamed x3, waiting for transfers between devices  387 us
    all_gather x1, waiting for transfers between devices, per_device(): everyone = lax.all_gather(stream, 'space', axis=1, tiled=True)  183 us
    ppermute x16, waiting for transfers between devices, from_behind(): lax.ppermute(value, axis, [(source, source + steps) for source in range(f...  61.7 us
    ppermute x16, starting transfers between devices, from_behind(): lax.ppermute(value, axis, [(source, source + steps) for source in range(f...  51 us
    dot_general x9, matrix products, attend(): jnp.einsum('tphd,spd->tphs', query_heads, pair_piece[:, :, 0, :], preferr...  22.3 us
  transfers between devices with their start and end apart: 21, of which 18 were waited for; matrix products, arithmetic and copies ran while one was open for 6% of the time, Pallas kernels for 0%

commit v1 on v0

v1 whole, which is shorter than its diff:
```python
import functools
import math

import jax
import jax.numpy as jnp
from jax import lax
from jax.experimental import pallas as pl
from jax.experimental.pallas import tpu as pltpu
from jax.sharding import PartitionSpec as P

MESH = pl.DeviceIdType.MESH
EPS = 1e-06
MASKED = -1e30
F32 = jnp.float32
BF16 = jnp.bfloat16
KINDS = ("q", "kv", "up", "o", "down")
N_SEMS = 144
TOKENS = 128
SUMS = 4


def device(core, x, y, z):
    return ((y * 2 + x // 2) * 2 + core, z * 2 + x % 2)


class Weight:
    def __init__(self, src, dst, along_rows):
        self.src, self.dst, self.along_rows = src, dst, along_rows
        self.size = src.shape[1] if along_rows else src.shape[0]

    def cut(self, ref, start, length, shard=None, shards=1):
        start = pl.multiple_of(start, 128)
        if shard is None:
            across = slice(None)
        elif isinstance(shard, int):
            across = slice(shard * self.size, (shard + shards) * self.size)
        else:
            step = 128 if self.along_rows else 16
            across = pl.ds(pl.multiple_of(shard * self.size, step), shards * self.size)
        if self.along_rows:
            return ref.at[pl.ds(start, length), across]
        return ref.at[across, pl.ds(start, length)]

    def own(self):
        return self.cut(self.dst, 0, 2048, 0)

    def src_half(self, core):
        return self.cut(self.src, core * 1024, 1024)

    def pair_half(self, core):
        return self.cut(self.dst, core * 1024, 1024, 1)

    def src_piece(self, core, y, x_hi):
        return self.cut(self.src, (core * 8 + y * 2 + x_hi) * 128, 128)

    def piece(self, core, y, x):
        return self.cut(self.dst, (core * 8 + y * 2 + x // 2) * 128, 128, 2 + x % 2)

    def region(self, core, y):
        return self.cut(self.dst, (core * 8 + y * 2) * 128, 256, 2, 2)

    def half_region(self, core, y, x_hi):
        return self.cut(self.dst, (core * 8 + y * 2 + x_hi) * 128, 128, 2, 2)


def root_scale(values, gain):
    return values * lax.rsqrt(jnp.mean(values * values, axis=-1, keepdims=True) + EPS) * gain


def kernel(
    frames, actions, table, norm_gain, wq, wkv, qk_gain, wo, wup, wdown, wlat, wconv, bias,
    out,
    frames_v, wq_v, wkv_v, wup_v, wo_v, wdown_v, wlat_v, wconv_v,
    x_v, n_v, q_v, qr_v, kvt_v, kvr_v, kvt_f, kvg_v, kvf_v, qn_v, ao_f, ao_v, at_v, h_v, p_v, pr_v,
    lat_v, lb_v, send_sem, recv_sem, local_sem,
):
    t, s = lax.axis_index("tm"), lax.axis_index("space")
    core, x_hi, y = t % 2, (t // 2) % 2, t // 4
    x_lo, z = s % 2, s // 2
    x = x_hi * 2 + x_lo
    other = 1 - core

    def at(dc=0, dx=0, dy=0, dz=0):
        return device((core + dc) % 2, (x + dx) % 4, (y + dy) % 4, (z + dz) % 8)

    above, below = (t, (s + 15) % 16), (t, (s + 1) % 16)
    barrier = pltpu.get_barrier_semaphore()
    near = [at(dz=1), at(dz=7), at(dz=2), at(dz=6), at(dz=4), at(dx=1), at(dx=3)]
    for partner in near + [above, below]:
        pl.semaphore_signal(barrier, inc=1, device_id=partner, device_id_type=MESH)

    def greet(step, carry):
        pl.semaphore_signal(
            barrier, inc=1, device_id=((t + step) % 16, s), device_id_type=MESH
        )
        return carry

    lax.fori_loop(1, 16, greet, 0)

    count = {"sem": 0, "local": 0}
    sent = []

    def take():
        count["sem"] += 1
        return count["sem"] - 1

    def remote(index, src, dst, target):
        return pltpu.make_async_remote_copy(
            src_ref=src, dst_ref=dst, send_sem=send_sem.at[index], recv_sem=recv_sem.at[index],
            device_id=target, device_id_type=MESH,
        )

    def push(index, src, dst, target):
        copy = remote(index, src, dst, target)
        copy.start()
        sent.append(copy)

    def arrive(index, dst):
        remote(index, dst, dst, (t, s)).wait_recv()

    def local(src, dst):
        copy = pltpu.make_async_copy(src, dst, local_sem.at[count["local"]])
        count["local"] += 1
        copy.start()
        return copy

    frames_copy = local(frames, frames_v)
    weights = {
        "q": Weight(wq, wq_v, True),
        "kv": Weight(wkv, wkv_v, False),
        "up": Weight(wup, wup_v, True),
        "o": Weight(wo, wo_v, False),
        "down": Weight(wdown, wdown_v, False),
    }
    own_copy = {kind: local(weights[kind].src, weights[kind].own()) for kind in KINDS}
    wlat_copy = local(wlat, wlat_v)
    wconv_copy = local(wconv, wconv_v)

    pl.semaphore_wait(barrier, 24)

    sems = {}

    def far_start(kind):
        w = weights[kind]
        sems[kind, "z"] = take()
        push(sems[kind, "z"], w.src_piece(core, y, x_hi), w.piece(core, y, x), at(dz=4))

    def pair_start(kind):
        w = weights[kind]
        sems[kind, "pair"] = take()
        target = device(core, (x + 3 + 2 * core) % 4, y, z)
        push(sems[kind, "pair"], w.src_half(core), w.pair_half(core), target)

    def pair_share(kind):
        w = weights[kind]
        arrive(sems[kind, "pair"], w.pair_half(core))
        sems[kind, "pair_c"] = take()
        push(sems[kind, "pair_c"], w.pair_half(core), w.pair_half(core), at(dc=1))

    def pair_done(kind):
        arrive(sems[kind, "pair_c"], weights[kind].pair_half(other))

    def row_start(kind):
        w = weights[kind]
        mine = w.piece(core, y, x)
        arrive(sems[kind, "z"], mine)
        for dx in (1, 3, 2):
            sems[kind, "x", dx] = take()
            push(sems[kind, "x", dx], mine, mine, at(dx=dx))

    def column_start(kind):
        w = weights[kind]
        for dx in (1, 3, 2):
            arrive(sems[kind, "x", dx], w.piece(core, y, (x + 4 - dx) % 4))
        mine = w.region(core, y)
        for dy in (1, 3):
            sems[kind, "y", dy] = take()
            push(sems[kind, "y", dy], mine, mine, at(dy=dy))
        sems[kind, "c", 0] = take()
        push(sems[kind, "c", 0], mine, mine, at(dc=1))

    def column_relay(kind):
        w = weights[kind]
        for dy, piece in ((1, 0), (3, 1)):
            row = (y + 4 - dy) % 4
            got = w.region(core, row)
            arrive(sems[kind, "y", dy], got)
            half = w.half_region(core, row, piece)
            sems[kind, "y2", dy] = take()
            push(sems[kind, "y2", dy], half, half, at(dy=dy))
            sems[kind, "c", dy] = take()
            push(sems[kind, "c", dy], got, got, at(dc=1))

    def column_end(kind):
        w = weights[kind]
        row = (y + 2) % 4
        for dy, piece in ((1, 0), (3, 1)):
            half = w.half_region(core, row, piece)
            arrive(sems[kind, "y2", dy], half)
            sems[kind, "c2", dy] = take()
            push(sems[kind, "c2", dy], half, half, at(dc=1))

    def far_done(kind):
        w = weights[kind]
        for dy in (0, 1, 3):
            arrive(sems[kind, "c", dy], w.region(other, (y + 4 - dy) % 4))
        for dy, piece in ((1, 0), (3, 1)):
            arrive(sems[kind, "c2", dy], w.half_region(other, (y + 2) % 4, piece))

    for kind in ("q", "kv"):
        far_start(kind)
        pair_start(kind)

    frames_copy.wait()
    row = lax.broadcasted_iota(jnp.int32, (TOKENS, TOKENS), 0)
    col = lax.broadcasted_iota(jnp.int32, (TOKENS, TOKENS), 1)
    turn = (col == (row & 7) * 16 + (row >> 3)).astype(F32).astype(BF16)
    moved = jnp.dot(turn, frames_v[...], preferred_element_type=F32)
    ids = actions[...]
    embedding = jnp.zeros((8, 2048), F32)
    for action in range(8):
        embedding += jnp.where(ids == action, table[action : action + 1, :].astype(F32), 0.0)
    stream = moved.reshape(16, 8, 2048) + embedding[None]
    x_v[0:128, :] = stream.reshape(TOKENS, 2048).astype(BF16)

    routes = (
        (1, slice(0, 128), slice(128, 256)),
        (7, slice(0, 128), slice(256, 384)),
        (2, slice(0, 64), slice(384, 448)),
        (6, slice(64, 128), slice(448, 512)),
    )
    token_sems = [take() for _ in routes]
    for index, (dz, home, away) in zip(token_sems, routes):
        push(index, x_v.at[home], x_v.at[away], at(dz=dz))
    for kind in ("up", "o", "down"):
        far_start(kind)
        pair_start(kind)

    def norm_block(index, carry):
        rows = pl.ds(pl.multiple_of(index * 16, 16), 16)
        n_v[rows, :] = root_scale(x_v[rows, :].astype(F32), norm_gain[...]).astype(BF16)
        return carry

    for kind in ("q", "kv"):
        row_start(kind)
    lax.fori_loop(0, 8, norm_block, 0)
    for kind in ("q", "kv"):
        column_start(kind)
        pair_share(kind)
    for kind in ("q", "kv"):
        column_relay(kind)
    row_start("up")
    for kind in ("q", "kv"):
        column_end(kind)
    column_start("up")
    for index, (dz, home, away) in zip(token_sems, routes):
        arrive(index, x_v.at[away])
    lax.fori_loop(8, 32, norm_block, 0)

    for kind in ("q", "kv"):
        own_copy[kind].wait()
        pair_done(kind)
        far_done(kind)
    for half in range(2):
        rows = slice(half * 256, half * 256 + 256)
        q_v[rows, :] = jnp.dot(n_v[rows, :], wq_v[...], preferred_element_type=F32).astype(BF16)
    kvt_v[...] = lax.dot_general(
        wkv_v[...], n_v[...], (((1,), (1,)), ((), ())), preferred_element_type=F32
    ).astype(BF16)
    kv_sems = [take() for _ in routes]
    kv_columns = (slice(128, 256), slice(256, 384), slice(384, 512), slice(384, 512))
    for slot, (index, (dz, home, away)) in enumerate(zip(kv_sems, routes)):
        push(index, kvt_v.at[:, kv_columns[slot]], kvr_v.at[slot], at(dz=8 - dz))
    q_sems = [take() for _ in routes]
    q_columns = (slice(512, 1024), slice(1024, 1536), slice(1536, 2048), slice(1536, 2048))
    for slot, (index, (dz, home, away)) in enumerate(zip(q_sems, routes)):
        push(index, q_v.at[away], qr_v.at[home, q_columns[slot]], at(dz=8 - dz))
    qr_v[:, 0:512] = q_v[0:128, :]

    def up_tiles(shard):
        def tile(index, carry):
            columns = pl.ds(pl.multiple_of(shard * 512 + index * 256, 256), 256)
            hidden = jnp.dot(n_v[...], wup_v[:, columns], preferred_element_type=F32)
            h_v[:, columns] = jax.nn.gelu(hidden, approximate=True).astype(BF16)
            return carry

        lax.fori_loop(0, 2, tile, 0)

    row_start("o")
    column_relay("up")
    row_start("down")
    column_start("o")
    own_copy["up"].wait()
    up_tiles(0)

    for slot, index in enumerate(kv_sems):
        arrive(index, kvr_v.at[slot])
    later_half = lax.broadcasted_iota(jnp.int32, (8, TOKENS), 1) >= 64
    for index, (plane, block) in enumerate((
        (z, kvt_v[:, 0:128].astype(F32)),
        (z + 1, kvr_v[0].astype(F32)),
        (z + 7, kvr_v[1].astype(F32)),
        (z + 2, kvr_v[2].astype(F32)),
        (z + 6, kvr_v[3].astype(F32)),
    )):
        near_plane, far_plane = plane % 8, (plane + 4) % 8
        places = (
            near_plane * 2 + x_lo,
            near_plane * 2 + 1 - x_lo,
            far_plane * 2,
            far_plane * 2 + 1,
        )
        for shard, place in enumerate(places):
            rows = pl.ds(pl.multiple_of(place * 8, 8), 8)
            for part in range(2):
                found = block[shard * 16 + part * 8 : shard * 16 + part * 8 + 8, :]
                if index == 4:
                    found = jnp.where(later_half, found, kvt_f[part, rows, :])
                kvt_f[part, rows, :] = found
    keys = root_scale(jnp.transpose(kvt_f[0]), qk_gain[1:2, :])
    values = jnp.transpose(kvt_f[1])
    kvg_v[t] = jnp.concatenate([keys, values], axis=1).astype(BF16)
    gather_sem = count["sem"]
    count["sem"] += 15

    def gather_send(step, carry):
        @pl.when(t + step < 16)
        def _():
            remote(
                gather_sem + step - 1, kvg_v.at[t], kvg_v.at[t], ((t + step) % 16, s)
            ).start()

        return carry

    def gather_wait(step, carry):
        @pl.when(t - step >= 0)
        def _():
            arrive(gather_sem + step - 1, kvg_v.at[(t + 16 - step) % 16])

        return carry

    def gather_sent(step, carry):
        @pl.when(t + step < 16)
        def _():
            remote(
                gather_sem + step - 1, kvg_v.at[t], kvg_v.at[t], ((t + step) % 16, s)
            ).wait_send()

        return carry

    lax.fori_loop(1, 16, gather_send, 0)

    column_end("up")
    pair_share("up")
    column_relay("o")
    column_start("down")

    for index, (slot, (dz, home, away)) in zip(q_sems, enumerate(routes)):
        arrive(index, qr_v.at[home, q_columns[slot]])
    for head in range(16):
        query = root_scale(qr_v[:, head * 128 : head * 128 + 128].astype(F32), qk_gain[0:1, :])
        qn_v[:, head] = query.astype(BF16).astype(F32).reshape(16, 8, 128)
    lax.fori_loop(1, 16, gather_wait, 0)

    def widen(index, carry):
        @pl.when(index <= t)
        def _():
            kvf_v[index] = kvg_v[index].astype(F32).reshape(16, 8, 256)

        @pl.when(index > t)
        def _():
            kvf_v[index] = jnp.zeros((16, 8, 256), F32)

        return carry

    lax.fori_loop(0, 16, widen, 0)
    allowed = col <= t * 8 + (row & 7)
    score_scale = 1.0 / math.sqrt(128)

    def attend(place, carry):
        query = qn_v[place].reshape(128, 128).astype(BF16)
        pair = kvf_v[:, place].reshape(128, 256).astype(BF16)
        scores = lax.dot_general(
            query, pair[:, 0:128], (((1,), (1,)), ((), ())), preferred_element_type=F32
        ) * score_scale
        scores = jnp.where(allowed, scores, MASKED)
        exponent = jnp.exp(scores - jnp.max(scores, axis=-1, keepdims=True))
        exponent = jnp.where(allowed, exponent, 0.0)
        totals = jnp.sum(exponent, axis=-1, keepdims=True)
        mixed = jnp.dot(exponent.astype(BF16), pair[:, 128:256], preferred_element_type=F32)
        mixed = mixed / totals
        rows = pl.ds(pl.multiple_of(place * 8, 8), 8)
        for head in range(16):
            ao_f[rows, head * 128 : head * 128 + 128] = mixed[head * 8 : head * 8 + 8, :]
        return carry

    lax.fori_loop(0, 16, attend, 0, unroll=2)
    ao_v[...] = ao_f[...].astype(BF16)
    at_v[0:128, :] = ao_v[:, 0:512]
    at_sems = [take() for _ in routes]
    for slot, (index, (dz, home, away)) in enumerate(zip(at_sems, routes)):
        push(index, ao_v.at[home, q_columns[slot]], at_v.at[away], at(dz=dz))

    column_end("o")
    column_relay("down")
    pair_done("up")
    up_tiles(1)
    pair_share("o")
    pair_share("down")
    column_end("down")
    far_done("up")
    up_tiles(2)
    up_tiles(3)
    for index, (dz, home, away) in zip(at_sems, routes):
        arrive(index, at_v.at[away])
    for kind in ("o", "down"):
        own_copy[kind].wait()
        pair_done(kind)
        far_done(kind)

    width = 2048 // SUMS
    sum_sems = []
    pr_places = ((0, slice(0, 128)), (1, slice(0, 128)), (2, slice(0, 64)), (2, slice(64, 128)))
    for chunk in range(SUMS):
        columns = slice(chunk * width, chunk * width + width)
        for half in range(2):
            rows = slice(half * 256, half * 256 + 256)
            part = jnp.dot(at_v[rows, :], wo_v[:, columns], preferred_element_type=F32)
            part += jnp.dot(h_v[rows, :], wdown_v[:, columns], preferred_element_type=F32)
            p_v[rows, columns] = part.astype(BF16)
        indices = [take() for _ in routes]
        sum_sems.append(indices)
        for slot, (index, (dz, home, away)) in enumerate(zip(indices, routes)):
            lead, span = pr_places[slot]
            push(index, p_v.at[away, columns], pr_v.at[lead, span, columns], at(dz=8 - dz))
    wlat_copy.wait()
    latent = jnp.zeros((TOKENS, 512), F32)
    for chunk in range(SUMS):
        columns = slice(chunk * width, chunk * width + width)
        for slot, index in enumerate(sum_sems[chunk]):
            lead, span = pr_places[slot]
            arrive(index, pr_v.at[lead, span, columns])
        total = p_v[0:128, columns].astype(F32)
        for lead in range(3):
            total += pr_v[lead, :, columns].astype(F32)
        block = (x_v[0:128, columns].astype(F32) + total).astype(BF16)
        latent += jnp.dot(block, wlat_v[columns, :], preferred_element_type=F32)
    lat_v[...] = (latent / (1.0 + jnp.exp(-latent))).astype(BF16)
    halo_sem = take()
    push(halo_sem, lat_v, lb_v, above)

    wconv_copy.wait()
    zero_rows = jnp.zeros((8, 512), F32)

    def right_of(cells):
        wide = cells.astype(F32)
        return jnp.concatenate([wide[8:, :], zero_rows], axis=0).astype(BF16)

    def tap(cells, down, across):
        return jnp.dot(cells, wconv_v[down, across], preferred_element_type=F32)

    o_row = lax.broadcasted_iota(jnp.int32, (256, 256), 0)
    o_col = lax.broadcasted_iota(jnp.int32, (256, 256), 1)
    weave = (o_col == (o_row & 1) * 128 + ((o_row >> 1) & 15) * 8 + (o_row >> 5)).astype(F32)
    weave = weave.astype(BF16)

    def store(parity, even, odd):
        pair = jnp.concatenate([even + bias[...], odd + bias[...]], axis=0).astype(BF16)
        woven = jnp.dot(weave, pair, preferred_element_type=F32).astype(BF16)
        out[:, parity] = woven.reshape(8, 32, 512)

    center = lat_v[...]
    right = right_of(center)
    store(0, tap(center, 1, 1), tap(right, 1, 0) + tap(center, 1, 2))
    odd_even = tap(center, 2, 1)
    odd_odd = tap(right, 2, 0) + tap(center, 2, 2)
    arrive(halo_sem, lb_v)
    under = jnp.where(s < 15, lb_v[...].astype(F32), 0.0).astype(BF16)
    corner = right_of(under)
    store(1, odd_even + tap(under, 0, 1), odd_odd + tap(corner, 0, 0) + tap(under, 0, 2))

    for copy in sent:
        copy.wait_send()
    lax.fori_loop(1, 16, gather_sent, 0)


def per_device(
    frames, actions, action_table, norm_gain, w_q, w_kv, qk_gain, w_o, w_up, w_down, w_lat, w_conv,
    conv_bias,
):
    w_kv = jnp.transpose(w_kv, (1, 2, 0)).reshape(16, 2048)
    vmem, anywhere = pl.BlockSpec(memory_space=pltpu.VMEM), pl.BlockSpec(memory_space=pl.ANY)
    flops = 2 * 512 * 2048 * (512 * 2 + 64 + 2048 * 2) + 2 * 128 * 512 * (2048 + 9 * 512)
    return pl.pallas_call(
        kernel,
        out_shape=jax.ShapeDtypeStruct((8, 2, 32, 512), BF16),
        in_specs=[
            anywhere, vmem, vmem, vmem, anywhere, anywhere, vmem, anywhere, anywhere, anywhere,
            anywhere, anywhere, vmem,
        ],
        out_specs=vmem,
        scratch_shapes=[
            pltpu.VMEM((128, 2048), BF16),
            pltpu.VMEM((2048, 512), BF16),
            pltpu.VMEM((64, 2048), BF16),
            pltpu.VMEM((2048, 2048), BF16),
            pltpu.VMEM((512, 2048), BF16),
            pltpu.VMEM((2048, 2048), BF16),
            pltpu.VMEM((2048, 512), BF16),
            pltpu.VMEM((3, 3, 512, 512), BF16),
            pltpu.VMEM((512, 2048), BF16),
            pltpu.VMEM((512, 2048), BF16),
            pltpu.VMEM((512, 512), BF16),
            pltpu.VMEM((128, 2048), BF16),
            pltpu.VMEM((64, 512), BF16),
            pltpu.VMEM((4, 64, 128), BF16),
            pltpu.VMEM((2, 128, 128), F32),
            pltpu.VMEM((16, 128, 256), BF16),
            pltpu.VMEM((16, 16, 8, 256), F32),
            pltpu.VMEM((16, 16, 8, 128), F32),
            pltpu.VMEM((128, 2048), F32),
            pltpu.VMEM((128, 2048), BF16),
            pltpu.VMEM((512, 512), BF16),
            pltpu.VMEM((512, 2048), BF16),
            pltpu.VMEM((512, 2048), BF16),
            pltpu.VMEM((3, 128, 2048), BF16),
            pltpu.VMEM((128, 512), BF16),
            pltpu.VMEM((128, 512), BF16),
            pltpu.SemaphoreType.DMA((N_SEMS,)),
            pltpu.SemaphoreType.DMA((N_SEMS,)),
            pltpu.SemaphoreType.DMA((8,)),
        ],
        compiler_params=pltpu.CompilerParams(
            collective_id=1, has_side_effects=True, vmem_limit_bytes=60 * 1024 * 1024
        ),
        cost_estimate=pl.CostEstimate(flops=flops, bytes_accessed=14000000, transcendentals=0),
        name="block",
    )(
        frames.reshape(128, 2048),
        actions.reshape(8, 1),
        action_table,
        norm_gain.reshape(1, 2048),
        w_q,
        w_kv,
        qk_gain,
        w_o,
        w_up,
        w_down,
        w_lat,
        w_conv,
        conv_bias.reshape(1, 512),
    )


def solution(mesh):
    return jax.shard_map(
        per_device,
        mesh=mesh,
        in_specs=(
            P("tm", "space", None, None),
            P("tm"),
            P(),
            P(),
            P(None, "space"),
            P(None, None, "space"),
            P(),
            P("space", None),
            P(None, "space"),
            P("space", None),
            P(),
            P(),
            P(),
        ),
        out_specs=P("tm", "space", None, None),
        check_vma=False,
    )
```

time: 911 us -> 151 us (0.17)
  waiting for transfers between devices: 636 us -> 0 us
  Pallas kernels: 0 us -> 147 us
  matrix products: 73.6 us -> 0 us
  starting transfers between devices: 71.9 us -> 0 us
  local copies, waits for them, and re-layouts: 65.6 us -> 3.2 us
  other arithmetic: 33.2 us -> 0 us
  between operations: 14.4 us -> 0.01 us
  loops' own time: 10.8 us -> 0 us
    unnamed x3 -> x0, waiting for transfers between devices: 387 us -> none
    all_gather x1 -> x0, waiting for transfers between devices: 183 us -> none  [per_device(): everyone = lax.all_gather(stream, 'space', axis=1, tiled=True)]
    pallas_call x0 -> x1, Pallas kernels: none -> 147 us  [per_device(): pl.pallas_call(kernel, out_shape=jax.ShapeDtypeStruct((8, 2, 32, 512), BF...]
    dot_general x28 -> x0, matrix products: 73.6 us -> none  [the longest x9 22.3 us: attend(): jnp.einsum('tphd,spd->tphs', query_heads, pair_piece[:, :, 0, :], preferr...]
    ppermute x16 -> x0, waiting for transfers between devices: 61.7 us -> none  [from_behind(): lax.ppermute(value, axis, [(source, source + steps) for source in range(f...]
    ppermute x16 -> x0, starting transfers between devices: 51 us -> none  [from_behind(): lax.ppermute(value, axis, [(source, source + steps) for source in range(f...]
    all_to_all x3 -> x0, starting transfers between devices: 20.6 us -> none  [the longest x1 8.48 us: per_device(): lax.all_to_all(pair_cols, 'space', split_axis=1, concat_axis=3, tiled=True)]
    unnamed x39 -> x1, local copies, waits for them, and re-layouts: 14.7 us -> 1.88 us
  transfers between devices with their start and end apart: 21 -> 0, of which waited for: 18 -> 0; matrix products, arithmetic and copies ran while one was open for 6% -> 0% of each run, Pallas kernels for 0% -> 0%
where the time goes in v1:
time: 151 us; the launch traced here: 150 us
  Pallas kernels  147 us (97%)
  local copies, waits for them, and re-layouts  3.2 us (2%)
    pallas_call x1, Pallas kernels, per_device(): pl.pallas_call(kernel, out_shape=jax.ShapeDtypeStruct((8, 2, 32, 512), BF...  147 us

profile of v1, /device:TPU:18, one launch (start us, length us, event | category | flops | bytes accessed | tf_op | source)
XLA Modules:
  0.0 150.1 jit_solution(15861830995450828821)
XLA Ops:
  0.0 1.3 copy.14.actions
  1.3 146.9 %block.1 = bf16[8,2,32,512]{3,2,1,0:T(8,128)(2,1)} custom-call(bf16[128,2048]{1,0:T(8,128)(2,1)} %bitcast.8, s32[8,1]{1,0:T(8,128)} %copy.14.actions, bf16[8,2048]{1,0:T(8,128)(2,1)} %table.1, f32[1,2048]{1,0:T(1,128)} %bitcast.10, bf16[2048,128]{1,0:T(8,128)(2,1)} %wq.1, bf16[16,2048]{1,0:T(8,128)(2,1)} %bitcast.9, f32[2,128]{1,0:T(2,128)} %qk_gain.1, ...), custom_call_target="tpu_custom_call" | custom-call | flops 11744051200 | bytes 14000000 | tf_op jit(solution)/shard_map/block/pallas_call | solution.py:494
  148.2 1.9 %copy.16 = bf16[8,2,32,512]{3,2,1,0:T(8,128)(2,1)} copy(bf16[8,2,32,512]{3,2,1,0:T(8,128)(2,1)} %block.1) | data formatting | bytes 1048576

commit v2 on v1

--- a/solution.py
+++ b/solution.py
@@ -71,7 +71,7 @@
     frames, actions, table, norm_gain, wq, wkv, qk_gain, wo, wup, wdown, wlat, wconv, bias,
     out,
     frames_v, wq_v, wkv_v, wup_v, wo_v, wdown_v, wlat_v, wconv_v,
-    x_v, n_v, q_v, qr_v, kvt_v, kvr_v, kvt_f, kvg_v, kvf_v, qn_v, ao_f, ao_v, at_v, h_v, p_v, pr_v,
+    x_v, n_v, q_v, qr_v, kvt_v, kvr_v, kvt_f, kvg_v, kvf_v, qn_v, ao_f, ao_v, at_v, h_v, p_v, pm_v, pr_v,
     lat_v, lb_v, send_sem, recv_sem, local_sem,
 ):
     t, s = lax.axis_index("tm"), lax.axis_index("space")
@@ -86,16 +86,16 @@
     above, below = (t, (s + 15) % 16), (t, (s + 1) % 16)
     barrier = pltpu.get_barrier_semaphore()
     near = [at(dz=1), at(dz=7), at(dz=2), at(dz=6), at(dz=4), at(dx=1), at(dx=3)]
-    for partner in near + [above, below]:
+    for partner in near + [above, below, at(dc=1)]:
         pl.semaphore_signal(barrier, inc=1, device_id=partner, device_id_type=MESH)
 
     def greet(step, carry):
         pl.semaphore_signal(
-            barrier, inc=1, device_id=((t + step) % 16, s), device_id_type=MESH
+            barrier, inc=1, device_id=((t + 2 * step) % 16, s), device_id_type=MESH
         )
         return carry
 
-    lax.fori_loop(1, 16, greet, 0)
+    lax.fori_loop(1, 8, greet, 0)
 
     count = {"sem": 0, "local": 0}
     sent = []
@@ -136,7 +136,7 @@
     wlat_copy = local(wlat, wlat_v)
     wconv_copy = local(wconv, wconv_v)
 
-    pl.semaphore_wait(barrier, 24)
+    pl.semaphore_wait(barrier, 17)
 
     sems = {}
 
@@ -207,8 +207,9 @@
         for dy, piece in ((1, 0), (3, 1)):
             arrive(sems[kind, "c2", dy], w.half_region(other, (y + 2) % 4, piece))
 
+    for kind in ("q", "kv", "up"):
+        far_start(kind)
     for kind in ("q", "kv"):
-        far_start(kind)
         pair_start(kind)
 
     frames_copy.wait()
@@ -216,54 +217,78 @@
     col = lax.broadcasted_iota(jnp.int32, (TOKENS, TOKENS), 1)
     turn = (col == (row & 7) * 16 + (row >> 3)).astype(F32).astype(BF16)
     moved = jnp.dot(turn, frames_v[...], preferred_element_type=F32)
-    ids = actions[...]
+    frame_row = lax.broadcasted_iota(jnp.int32, (8, 2048), 0)
+    ids = jnp.zeros((8, 2048), jnp.int32)
+    for frame in range(8):
+        ids = jnp.where(frame_row == frame, actions[frame], ids)
     embedding = jnp.zeros((8, 2048), F32)
     for action in range(8):
         embedding += jnp.where(ids == action, table[action : action + 1, :].astype(F32), 0.0)
     stream = moved.reshape(16, 8, 2048) + embedding[None]
     x_v[0:128, :] = stream.reshape(TOKENS, 2048).astype(BF16)
 
+    token_sems = {}
+
+    def token_send(name, home, away, dz):
+        token_sems[name] = take()
+        push(token_sems[name], x_v.at[home], x_v.at[away], at(dz=dz))
+
+    token_send("up first", slice(0, 64), slice(128, 192), 1)
+    token_send("down last", slice(64, 128), slice(320, 384), 7)
+    token_send("up last", slice(64, 128), slice(192, 256), 1)
+    token_send("down first", slice(0, 64), slice(256, 320), 7)
+
+    def token_arrive(name, away):
+        arrive(token_sems[name], x_v.at[away])
+
+    def norm_rows(first, last):
+        def block(index, carry):
+            rows = pl.ds(pl.multiple_of(index * 16, 16), 16)
+            n_v[rows, :] = root_scale(x_v[rows, :].astype(F32), norm_gain[...]).astype(BF16)
+            return carry
+
+        lax.fori_loop(first // 16, last // 16, block, 0)
+
+    for kind in ("q", "kv"):
+        row_start(kind)
+    norm_rows(0, 128)
+    row_start("up")
+    for kind in ("o", "down"):
+        far_start(kind)
+    for kind in ("q", "kv"):
+        column_start(kind)
+    pair_start("up")
+    token_arrive("up first", slice(128, 192))
+    token_send("up on", slice(128, 192), slice(384, 448), 1)
+    token_arrive("down last", slice(320, 384))
+    token_send("down on", slice(320, 384), slice(448, 512), 7)
+    column_start("up")
+    for kind in ("q", "kv"):
+        pair_share(kind)
+        column_relay(kind)
+    for kind in ("q", "kv"):
+        column_end(kind)
+    token_arrive("up last", slice(192, 256))
+    token_arrive("down first", slice(256, 320))
+    norm_rows(128, 384)
+    row_start("o")
+    row_start("down")
+    for kind in ("o", "down"):
+        pair_start(kind)
+    token_arrive("up on", slice(384, 448))
+    token_arrive("down on", slice(448, 512))
+    norm_rows(384, 512)
+
+    for kind in ("q", "kv"):
+        own_copy[kind].wait()
+        pair_done(kind)
+        far_done(kind)
     routes = (
         (1, slice(0, 128), slice(128, 256)),
         (7, slice(0, 128), slice(256, 384)),
         (2, slice(0, 64), slice(384, 448)),
         (6, slice(64, 128), slice(448, 512)),
     )
-    token_sems = [take() for _ in routes]
-    for index, (dz, home, away) in zip(token_sems, routes):
-        push(index, x_v.at[home], x_v.at[away], at(dz=dz))
-    for kind in ("up", "o", "down"):
-        far_start(kind)
-        pair_start(kind)
-
-    def norm_block(index, carry):
-        rows = pl.ds(pl.multiple_of(index * 16, 16), 16)
-        n_v[rows, :] = root_scale(x_v[rows, :].astype(F32), norm_gain[...]).astype(BF16)
-        return carry
-
-    for kind in ("q", "kv"):
-        row_start(kind)
-    lax.fori_loop(0, 8, norm_block, 0)
-    for kind in ("q", "kv"):
-        column_start(kind)
-        pair_share(kind)
-    for kind in ("q", "kv"):
-        column_relay(kind)
-    row_start("up")
-    for kind in ("q", "kv"):
-        column_end(kind)
-    column_start("up")
-    for index, (dz, home, away) in zip(token_sems, routes):
-        arrive(index, x_v.at[away])
-    lax.fori_loop(8, 32, norm_block, 0)
-
-    for kind in ("q", "kv"):
-        own_copy[kind].wait()
-        pair_done(kind)
-        far_done(kind)
-    for half in range(2):
-        rows = slice(half * 256, half * 256 + 256)
-        q_v[rows, :] = jnp.dot(n_v[rows, :], wq_v[...], preferred_element_type=F32).astype(BF16)
     kvt_v[...] = lax.dot_general(
         wkv_v[...], n_v[...], (((1,), (1,)), ((), ())), preferred_element_type=F32
     ).astype(BF16)
@@ -271,6 +296,9 @@
     kv_columns = (slice(128, 256), slice(256, 384), slice(384, 512), slice(384, 512))
     for slot, (index, (dz, home, away)) in enumerate(zip(kv_sems, routes)):
         push(index, kvt_v.at[:, kv_columns[slot]], kvr_v.at[slot], at(dz=8 - dz))
+    for half in range(2):
+        rows = slice(half * 256, half * 256 + 256)
+        q_v[rows, :] = jnp.dot(n_v[rows, :], wq_v[...], preferred_element_type=F32).astype(BF16)
     q_sems = [take() for _ in routes]
     q_columns = (slice(512, 1024), slice(1024, 1536), slice(1536, 2048), slice(1536, 2048))
     for slot, (index, (dz, home, away)) in enumerate(zip(q_sems, routes)):
@@ -286,10 +314,9 @@
 
         lax.fori_loop(0, 2, tile, 0)
 
-    row_start("o")
+    column_start("o")
     column_relay("up")
-    row_start("down")
-    column_start("o")
+    column_start("down")
     own_copy["up"].wait()
     up_tiles(0)
 
@@ -320,47 +347,76 @@
     keys = root_scale(jnp.transpose(kvt_f[0]), qk_gain[1:2, :])
     values = jnp.transpose(kvt_f[1])
     kvg_v[t] = jnp.concatenate([keys, values], axis=1).astype(BF16)
-    gather_sem = count["sem"]
+    chip = t // 2
+    gather_sem, share_sem = count["sem"], count["sem"] + 7
     count["sem"] += 15
 
+    def gather(step):
+        mine = kvg_v.at[t]
+        return remote(gather_sem + step - 1, mine, mine, ((t + 2 * step) % 16, s))
+
+    def share(step):
+        got = kvg_v.at[(t + 16 - 2 * step) % 16]
+        return remote(share_sem + step, got, got, at(dc=1))
+
     def gather_send(step, carry):
-        @pl.when(t + step < 16)
+        @pl.when(chip + step < 8)
         def _():
-            remote(
-                gather_sem + step - 1, kvg_v.at[t], kvg_v.at[t], ((t + step) % 16, s)
-            ).start()
+            gather(step).start()
 
         return carry
 
+    def gather_pass(step, carry):
+        @pl.when(chip - step >= 0)
+        def _():
+            arrive(gather_sem + step - 1, kvg_v.at[(t + 16 - 2 * step) % 16])
+            share(step).start()
+
+        return carry
+
     def gather_wait(step, carry):
-        @pl.when(t - step >= 0)
+        @pl.when(chip - step >= 0)
         def _():
-            arrive(gather_sem + step - 1, kvg_v.at[(t + 16 - step) % 16])
+            arrive(share_sem + step, kvg_v.at[(t + 16 - 2 * step + 1 - 2 * core) % 16])
 
         return carry
 
     def gather_sent(step, carry):
-        @pl.when(t + step < 16)
+        @pl.when(chip + step < 8)
         def _():
-            remote(
-                gather_sem + step - 1, kvg_v.at[t], kvg_v.at[t], ((t + step) % 16, s)
-            ).wait_send()
+            gather(step).wait_send()
+
+        @pl.when(chip - step >= 0)
+        def _():
+            share(step).wait_send()
 
         return carry
 
-    lax.fori_loop(1, 16, gather_send, 0)
+    lax.fori_loop(1, 8, gather_send, 0)
+
+    @pl.when(core == 0)
+    def _():
+        share(0).start()
 
     column_end("up")
     pair_share("up")
     column_relay("o")
-    column_start("down")
+    pair_done("up")
+    up_tiles(1)
+    column_relay("down")
 
     for index, (slot, (dz, home, away)) in zip(q_sems, enumerate(routes)):
         arrive(index, qr_v.at[home, q_columns[slot]])
     for head in range(16):
         query = root_scale(qr_v[:, head * 128 : head * 128 + 128].astype(F32), qk_gain[0:1, :])
         qn_v[:, head] = query.astype(BF16).astype(F32).reshape(16, 8, 128)
-    lax.fori_loop(1, 16, gather_wait, 0)
+    lax.fori_loop(1, 8, gather_pass, 0)
+
+    @pl.when(core == 1)
+    def _():
+        arrive(share_sem, kvg_v.at[t - 1])
+
+    lax.fori_loop(1, 8, gather_wait, 0)
 
     def widen(index, carry):
         @pl.when(index <= t)
@@ -400,13 +456,9 @@
     at_sems = [take() for _ in routes]
     for slot, (index, (dz, home, away)) in enumerate(zip(at_sems, routes)):
         push(index, ao_v.at[home, q_columns[slot]], at_v.at[away], at(dz=dz))
-
-    column_end("o")
-    column_relay("down")
-    pair_done("up")
-    up_tiles(1)
     pair_share("o")
     pair_share("down")
+    column_end("o")
     column_end("down")
     far_done("up")
     up_tiles(2)
@@ -419,30 +471,48 @@
         far_done(kind)
 
     width = 2048 // SUMS
-    sum_sems = []
-    pr_places = ((0, slice(0, 128)), (1, slice(0, 128)), (2, slice(0, 64)), (2, slice(64, 128)))
-    for chunk in range(SUMS):
-        columns = slice(chunk * width, chunk * width + width)
-        for half in range(2):
+    half_sems, sum_sems = [], []
+    merges = ((7, slice(384, 448), slice(128, 192)), (1, slice(448, 512), slice(320, 384)))
+
+    def chunk_of(chunk):
+        return slice(chunk * width, chunk * width + width)
+
+    def multiply(chunk):
+        columns = chunk_of(chunk)
+        for half in (1, 0):
             rows = slice(half * 256, half * 256 + 256)
             part = jnp.dot(at_v[rows, :], wo_v[:, columns], preferred_element_type=F32)
             part += jnp.dot(h_v[rows, :], wdown_v[:, columns], preferred_element_type=F32)
             p_v[rows, columns] = part.astype(BF16)
-        indices = [take() for _ in routes]
+        indices = [take() for _ in merges]
+        half_sems.append(indices)
+        for side, (index, (dz, away, near_rows)) in enumerate(zip(indices, merges)):
+            push(index, p_v.at[away, columns], pm_v.at[side, :, columns], at(dz=dz))
+
+    def merge(chunk):
+        columns = chunk_of(chunk)
+        for side, (dz, away, near_rows) in enumerate(merges):
+            arrive(half_sems[chunk][side], pm_v.at[side, :, columns])
+            both = p_v[near_rows, columns].astype(F32) + pm_v[side, :, columns].astype(F32)
+            p_v[near_rows, columns] = both.astype(BF16)
+        indices = [take() for _ in range(2)]
         sum_sems.append(indices)
-        for slot, (index, (dz, home, away)) in enumerate(zip(indices, routes)):
-            lead, span = pr_places[slot]
-            push(index, p_v.at[away, columns], pr_v.at[lead, span, columns], at(dz=8 - dz))
+        for side, (dz, rows) in enumerate(((7, slice(128, 256)), (1, slice(256, 384)))):
+            push(indices[side], p_v.at[rows, columns], pr_v.at[side, :, columns], at(dz=dz))
+
+    multiply(0)
+    for chunk in range(1, SUMS):
+        multiply(chunk)
+        merge(chunk - 1)
+    merge(SUMS - 1)
     wlat_copy.wait()
     latent = jnp.zeros((TOKENS, 512), F32)
     for chunk in range(SUMS):
-        columns = slice(chunk * width, chunk * width + width)
-        for slot, index in enumerate(sum_sems[chunk]):
-            lead, span = pr_places[slot]
-            arrive(index, pr_v.at[lead, span, columns])
+        columns = chunk_of(chunk)
         total = p_v[0:128, columns].astype(F32)
-        for lead in range(3):
-            total += pr_v[lead, :, columns].astype(F32)
+        for side in range(2):
+            arrive(sum_sems[chunk][side], pr_v.at[side, :, columns])
+            total += pr_v[side, :, columns].astype(F32)
         block = (x_v[0:128, columns].astype(F32) + total).astype(BF16)
         latent += jnp.dot(block, wlat_v[columns, :], preferred_element_type=F32)
     lat_v[...] = (latent / (1.0 + jnp.exp(-latent))).astype(BF16)
@@ -481,7 +551,12 @@
 
     for copy in sent:
         copy.wait_send()
-    lax.fori_loop(1, 16, gather_sent, 0)
+
+    @pl.when(core == 0)
+    def _():
+        share(0).wait_send()
+
+    lax.fori_loop(1, 8, gather_sent, 0)
 
 
 def per_device(
@@ -490,12 +565,13 @@
 ):
     w_kv = jnp.transpose(w_kv, (1, 2, 0)).reshape(16, 2048)
     vmem, anywhere = pl.BlockSpec(memory_space=pltpu.VMEM), pl.BlockSpec(memory_space=pl.ANY)
+    smem = pl.BlockSpec(memory_space=pltpu.SMEM)
     flops = 2 * 512 * 2048 * (512 * 2 + 64 + 2048 * 2) + 2 * 128 * 512 * (2048 + 9 * 512)
     return pl.pallas_call(
         kernel,
         out_shape=jax.ShapeDtypeStruct((8, 2, 32, 512), BF16),
         in_specs=[
-            anywhere, vmem, vmem, vmem, anywhere, anywhere, vmem, anywhere, anywhere, anywhere,
+            anywhere, smem, vmem, vmem, anywhere, anywhere, vmem, anywhere, anywhere, anywhere,
             anywhere, anywhere, vmem,
         ],
         out_specs=vmem,
@@ -523,7 +599,8 @@
             pltpu.VMEM((512, 512), BF16),
             pltpu.VMEM((512, 2048), BF16),
             pltpu.VMEM((512, 2048), BF16),
-            pltpu.VMEM((3, 128, 2048), BF16),
+            pltpu.VMEM((2, 64, 2048), BF16),
+            pltpu.VMEM((2, 128, 2048), BF16),
             pltpu.VMEM((128, 512), BF16),
             pltpu.VMEM((128, 512), BF16),
             pltpu.SemaphoreType.DMA((N_SEMS,)),
@@ -537,7 +614,7 @@
         name="block",
     )(
         frames.reshape(128, 2048),
-        actions.reshape(8, 1),
+        actions,
         action_table,
         norm_gain.reshape(1, 2048),
         w_q,

time: 151 us -> 122 us (0.81)
  Pallas kernels: 147 us -> 120 us
    pallas_call x1, Pallas kernels: 147 us -> 120 us  [per_device(): pl.pallas_call(kernel, out_shape=jax.ShapeDtypeStruct((8, 2, 32, 512), BF...]
where the time goes in v2:
time: 122 us
  Pallas kernels  120 us (98%)
  local copies, waits for them, and re-layouts  1.88 us (2%)
    pallas_call x1, Pallas kernels, per_device(): pl.pallas_call(kernel, out_shape=jax.ShapeDtypeStruct((8, 2, 32, 512), BF...  120 us

profile of v2, /device:TPU:18, one launch (start us, length us, event | category | flops | bytes accessed | tf_op | source)
XLA Modules:
  0.0 121.7 jit_solution(381068805251937719)
XLA Ops:
  0.0 119.8 %block.1 = bf16[8,2,32,512]{3,2,1,0:T(8,128)(2,1)} custom-call(bf16[128,2048]{1,0:T(8,128)(2,1)} %bitcast.6, s32[8]{0:T(128)} %actions.1, bf16[8,2048]{1,0:T(8,128)(2,1)} %table.1, f32[1,2048]{1,0:T(1,128)} %bitcast.8, bf16[2048,128]{1,0:T(8,128)(2,1)} %wq.1, bf16[16,2048]{1,0:T(8,128)(2,1)} %bitcast.7, f32[2,128]{1,0:T(2,128)} %qk_gain.1, ...), custom_call_target="tpu_custom_call" | custom-call | flops 11744051200 | bytes 14000000 | tf_op jit(solution)/shard_map/block/pallas_call | solution.py:570
  119.8 1.9 %copy.15 = bf16[8,2,32,512]{3,2,1,0:T(8,128)(2,1)} copy(bf16[8,2,32,512]{3,2,1,0:T(8,128)(2,1)} %block.1) | data formatting | bytes 1048576

commit v3 on v2

--- a/solution.py
+++ b/solution.py
@@ -13,10 +13,9 @@
 MASKED = -1e30
 F32 = jnp.float32
 BF16 = jnp.bfloat16
-KINDS = ("q", "kv", "up", "o", "down")
-N_SEMS = 144
+KINDS = ("q", "kv", "up", "od")
+N_SEMS = 112
 TOKENS = 128
-SUMS = 4
 
 
 def device(core, x, y, z):
@@ -63,6 +62,41 @@
         return self.cut(self.dst, (core * 8 + y * 2 + x_hi) * 128, 128, 2, 2)
 
 
+class Folded(Weight):
+    def __init__(self, src, dst):
+        self.src, self.dst = src, dst
+
+    def own(self):
+        return self.dst.at[0]
+
+    def src_half(self, core):
+        return self.src.at[pl.ds(pl.multiple_of(core * 320, 320), 320)]
+
+    def pair_half(self, core):
+        return self.dst.at[1, pl.ds(pl.multiple_of(core * 320, 320), 320)]
+
+    def block(self, core, y):
+        rows = pl.ds(pl.multiple_of((core * 2 + y // 2) * 160, 160), 160)
+        return rows, (y % 2) * 256
+
+    def src_piece(self, core, y, x_hi):
+        rows, column = self.block(core, y)
+        return self.src.at[rows, pl.ds(pl.multiple_of(column + x_hi * 128, 128), 128)]
+
+    def piece(self, core, y, x):
+        rows, column = self.block(core, y)
+        columns = pl.ds(pl.multiple_of(column + x // 2 * 128, 128), 128)
+        return self.dst.at[2 + x % 2, rows, columns]
+
+    def region(self, core, y):
+        rows, column = self.block(core, y)
+        return self.dst.at[2:4, rows, pl.ds(pl.multiple_of(column, 256), 256)]
+
+    def half_region(self, core, y, x_hi):
+        rows, column = self.block(core, y)
+        return self.dst.at[2:4, rows, pl.ds(pl.multiple_of(column + x_hi * 128, 128), 128)]
+
+
 def root_scale(values, gain):
     return values * lax.rsqrt(jnp.mean(values * values, axis=-1, keepdims=True) + EPS) * gain
 
@@ -70,8 +104,8 @@
 def kernel(
     frames, actions, table, norm_gain, wq, wkv, qk_gain, wo, wup, wdown, wlat, wconv, bias,
     out,
-    frames_v, wq_v, wkv_v, wup_v, wo_v, wdown_v, wlat_v, wconv_v,
-    x_v, n_v, q_v, qr_v, kvt_v, kvr_v, kvt_f, kvg_v, kvf_v, qn_v, ao_f, ao_v, at_v, h_v, p_v, pm_v, pr_v,
+    frames_v, wq_v, wkv_v, wup_v, wo_v, wdown_v, wlat_v, wconv_v, od_v, ods_v,
+    x_v, n_v, q_v, qr_v, kvt_v, kvr_v, kvt_f, kvg_v, kvf_v, qn_v, ao_f, ao_v, at_v, h_v, p_v, pr_v, ffn_f,
     lat_v, lb_v, send_sem, recv_sem, local_sem,
 ):
     t, s = lax.axis_index("tm"), lax.axis_index("space")
@@ -129,11 +163,10 @@
         "q": Weight(wq, wq_v, True),
         "kv": Weight(wkv, wkv_v, False),
         "up": Weight(wup, wup_v, True),
-        "o": Weight(wo, wo_v, False),
-        "down": Weight(wdown, wdown_v, False),
+        "od": Folded(od_v, ods_v),
     }
-    own_copy = {kind: local(weights[kind].src, weights[kind].own()) for kind in KINDS}
-    wlat_copy = local(wlat, wlat_v)
+    fold_copies = [local(wlat, wlat_v), local(wo, wo_v), local(wdown, wdown_v)]
+    own_copy = {kind: local(weights[kind].src, weights[kind].own()) for kind in ("q", "kv", "up")}
     wconv_copy = local(wconv, wconv_v)
 
     pl.semaphore_wait(barrier, 17)
@@ -173,7 +206,7 @@
         for dx in (1, 3, 2):
             arrive(sems[kind, "x", dx], w.piece(core, y, (x + 4 - dx) % 4))
         mine = w.region(core, y)
-        for dy in (1, 3):
+        for dy in (1, 3) if kind == "up" else (1, 3, 2):
             sems[kind, "y", dy] = take()
             push(sems[kind, "y", dy], mine, mine, at(dy=dy))
         sems[kind, "c", 0] = take()
@@ -191,6 +224,14 @@
             sems[kind, "c", dy] = take()
             push(sems[kind, "c", dy], got, got, at(dc=1))
 
+    def column_share(kind):
+        w = weights[kind]
+        for dy in (1, 3, 2):
+            got = w.region(core, (y + 4 - dy) % 4)
+            arrive(sems[kind, "y", dy], got)
+            sems[kind, "c", dy] = take()
+            push(sems[kind, "c", dy], got, got, at(dc=1))
+
     def column_end(kind):
         w = weights[kind]
         row = (y + 2) % 4
@@ -202,12 +243,12 @@
 
     def far_done(kind):
         w = weights[kind]
-        for dy in (0, 1, 3):
+        for dy in (0, 1, 3) if kind == "up" else (0, 1, 3, 2):
             arrive(sems[kind, "c", dy], w.region(other, (y + 4 - dy) % 4))
-        for dy, piece in ((1, 0), (3, 1)):
+        for dy, piece in ((1, 0), (3, 1)) if kind == "up" else ():
             arrive(sems[kind, "c2", dy], w.half_region(other, (y + 2) % 4, piece))
 
-    for kind in ("q", "kv", "up"):
+    for kind in ("q", "kv"):
         far_start(kind)
     for kind in ("q", "kv"):
         pair_start(kind)
@@ -235,8 +276,6 @@
 
     token_send("up first", slice(0, 64), slice(128, 192), 1)
     token_send("down last", slice(64, 128), slice(320, 384), 7)
-    token_send("up last", slice(64, 128), slice(192, 256), 1)
-    token_send("down first", slice(0, 64), slice(256, 320), 7)
 
     def token_arrive(name, away):
         arrive(token_sems[name], x_v.at[away])
@@ -249,32 +288,36 @@
 
         lax.fori_loop(first // 16, last // 16, block, 0)
 
+    for copy in fold_copies:
+        copy.wait()
+    od_v[0:128, :] = jnp.dot(wo_v[...], wlat_v[...], preferred_element_type=F32).astype(BF16)
+    od_v[128:640, :] = jnp.dot(wdown_v[...], wlat_v[...], preferred_element_type=F32).astype(BF16)
+    token_send("up last", slice(64, 128), slice(192, 256), 1)
+    token_send("down first", slice(0, 64), slice(256, 320), 7)
+    for kind in ("up", "od"):
+        far_start(kind)
     for kind in ("q", "kv"):
         row_start(kind)
+    ods_v[0] = od_v[...]
     norm_rows(0, 128)
-    row_start("up")
-    for kind in ("o", "down"):
-        far_start(kind)
-    for kind in ("q", "kv"):
-        column_start(kind)
-    pair_start("up")
     token_arrive("up first", slice(128, 192))
     token_send("up on", slice(128, 192), slice(384, 448), 1)
     token_arrive("down last", slice(320, 384))
     token_send("down on", slice(320, 384), slice(448, 512), 7)
-    column_start("up")
+    for kind in ("q", "kv"):
+        column_start(kind)
     for kind in ("q", "kv"):
         pair_share(kind)
-        column_relay(kind)
+    pair_start("up")
     for kind in ("q", "kv"):
-        column_end(kind)
+        column_share(kind)
     token_arrive("up last", slice(192, 256))
     token_arrive("down first", slice(256, 320))
+    row_start("up")
     norm_rows(128, 384)
-    row_start("o")
-    row_start("down")
-    for kind in ("o", "down"):
-        pair_start(kind)
+    pair_start("od")
+    row_start("od")
+    column_start("up")
     token_arrive("up on", slice(384, 448))
     token_arrive("down on", slice(448, 512))
     norm_rows(384, 512)
@@ -314,11 +357,10 @@
 
         lax.fori_loop(0, 2, tile, 0)
 
-    column_start("o")
-    column_relay("up")
-    column_start("down")
+    column_start("od")
     own_copy["up"].wait()
     up_tiles(0)
+    pair_share("up")
 
     for slot, index in enumerate(kv_sems):
         arrive(index, kvr_v.at[slot])
@@ -398,12 +440,10 @@
     def _():
         share(0).start()
 
-    column_end("up")
-    pair_share("up")
-    column_relay("o")
+    column_relay("up")
     pair_done("up")
     up_tiles(1)
-    column_relay("down")
+    column_share("od")
 
     for index, (slot, (dz, home, away)) in zip(q_sems, enumerate(routes)):
         arrive(index, qr_v.at[home, q_columns[slot]])
@@ -456,65 +496,47 @@
     at_sems = [take() for _ in routes]
     for slot, (index, (dz, home, away)) in enumerate(zip(at_sems, routes)):
         push(index, ao_v.at[home, q_columns[slot]], at_v.at[away], at(dz=dz))
-    pair_share("o")
-    pair_share("down")
-    column_end("o")
-    column_end("down")
+    column_end("up")
+    pair_share("od")
     far_done("up")
     up_tiles(2)
     up_tiles(3)
+    pair_done("od")
+    far_done("od")
+
+    for half in (1, 0):
+        rows = slice(half * 256, half * 256 + 256)
+        ffn = jnp.zeros((256, 512), F32)
+        for shard in range(4):
+            ffn += jnp.dot(
+                h_v[rows, shard * 512 : shard * 512 + 512], ods_v[shard, 128:640, :],
+                preferred_element_type=F32,
+            )
+        ffn_f[rows, :] = ffn
     for index, (dz, home, away) in zip(at_sems, routes):
         arrive(index, at_v.at[away])
-    for kind in ("o", "down"):
-        own_copy[kind].wait()
-        pair_done(kind)
-        far_done(kind)
-
-    width = 2048 // SUMS
-    half_sems, sum_sems = [], []
-    merges = ((7, slice(384, 448), slice(128, 192)), (1, slice(448, 512), slice(320, 384)))
-
-    def chunk_of(chunk):
-        return slice(chunk * width, chunk * width + width)
-
-    def multiply(chunk):
-        columns = chunk_of(chunk)
-        for half in (1, 0):
-            rows = slice(half * 256, half * 256 + 256)
-            part = jnp.dot(at_v[rows, :], wo_v[:, columns], preferred_element_type=F32)
-            part += jnp.dot(h_v[rows, :], wdown_v[:, columns], preferred_element_type=F32)
-            p_v[rows, columns] = part.astype(BF16)
-        indices = [take() for _ in merges]
-        half_sems.append(indices)
-        for side, (index, (dz, away, near_rows)) in enumerate(zip(indices, merges)):
-            push(index, p_v.at[away, columns], pm_v.at[side, :, columns], at(dz=dz))
-
-    def merge(chunk):
-        columns = chunk_of(chunk)
-        for side, (dz, away, near_rows) in enumerate(merges):
-            arrive(half_sems[chunk][side], pm_v.at[side, :, columns])
-            both = p_v[near_rows, columns].astype(F32) + pm_v[side, :, columns].astype(F32)
-            p_v[near_rows, columns] = both.astype(BF16)
-        indices = [take() for _ in range(2)]
-        sum_sems.append(indices)
-        for side, (dz, rows) in enumerate(((7, slice(128, 256)), (1, slice(256, 384)))):
-            push(indices[side], p_v.at[rows, columns], pr_v.at[side, :, columns], at(dz=dz))
-
-    multiply(0)
-    for chunk in range(1, SUMS):
-        multiply(chunk)
-        merge(chunk - 1)
-    merge(SUMS - 1)
-    wlat_copy.wait()
-    latent = jnp.zeros((TOKENS, 512), F32)
-    for chunk in range(SUMS):
-        columns = chunk_of(chunk)
-        total = p_v[0:128, columns].astype(F32)
-        for side in range(2):
-            arrive(sum_sems[chunk][side], pr_v.at[side, :, columns])
-            total += pr_v[side, :, columns].astype(F32)
-        block = (x_v[0:128, columns].astype(F32) + total).astype(BF16)
-        latent += jnp.dot(block, wlat_v[columns, :], preferred_element_type=F32)
+    sum_sems = [take() for _ in routes]
+    places = ((0, slice(0, 128)), (1, slice(0, 128)), (2, slice(0, 64)), (2, slice(64, 128)))
+    for half in (1, 0):
+        rows = slice(half * 256, half * 256 + 256)
+        part = ffn_f[rows, :]
+        for shard in range(4):
+            part += jnp.dot(
+                at_v[rows, shard * 128 : shard * 128 + 128], ods_v[shard, 0:128, :],
+                preferred_element_type=F32,
+            )
+        p_v[rows, :] = part.astype(BF16)
+        for slot in ((2, 3, 1), (0,))[1 - half]:
+            dz, home, away = routes[slot]
+            lead, span = places[slot]
+            push(sum_sems[slot], p_v.at[away], pr_v.at[lead, span], at(dz=8 - dz))
+    latent = jnp.dot(x_v[0:128, :], wlat_v[...], preferred_element_type=F32)
+    latent += p_v[0:128, :].astype(F32)
+    for slot, index in enumerate(sum_sems):
+        lead, span = places[slot]
+        arrive(index, pr_v.at[lead, span])
+    for lead in range(3):
+        latent += pr_v[lead].astype(F32)
     lat_v[...] = (latent / (1.0 + jnp.exp(-latent))).astype(BF16)
     halo_sem = take()
     push(halo_sem, lat_v, lb_v, above)
@@ -566,7 +588,7 @@
     w_kv = jnp.transpose(w_kv, (1, 2, 0)).reshape(16, 2048)
     vmem, anywhere = pl.BlockSpec(memory_space=pltpu.VMEM), pl.BlockSpec(memory_space=pl.ANY)
     smem = pl.BlockSpec(memory_space=pltpu.SMEM)
-    flops = 2 * 512 * 2048 * (512 * 2 + 64 + 2048 * 2) + 2 * 128 * 512 * (2048 + 9 * 512)
+    flops = 2 * 512 * 2048 * (512 * 2 + 64 + 2048 + 512) + 2 * 128 * 512 * (2048 + 9 * 512)
     return pl.pallas_call(
         kernel,
         out_shape=jax.ShapeDtypeStruct((8, 2, 32, 512), BF16),
@@ -580,10 +602,12 @@
             pltpu.VMEM((2048, 512), BF16),
             pltpu.VMEM((64, 2048), BF16),
             pltpu.VMEM((2048, 2048), BF16),
+            pltpu.VMEM((128, 2048), BF16),
             pltpu.VMEM((512, 2048), BF16),
-            pltpu.VMEM((2048, 2048), BF16),
             pltpu.VMEM((2048, 512), BF16),
             pltpu.VMEM((3, 3, 512, 512), BF16),
+            pltpu.VMEM((640, 512), BF16),
+            pltpu.VMEM((4, 640, 512), BF16),
             pltpu.VMEM((512, 2048), BF16),
             pltpu.VMEM((512, 2048), BF16),
             pltpu.VMEM((512, 512), BF16),
@@ -598,9 +622,9 @@
             pltpu.VMEM((128, 2048), BF16),
             pltpu.VMEM((512, 512), BF16),
             pltpu.VMEM((512, 2048), BF16),
-            pltpu.VMEM((512, 2048), BF16),
-            pltpu.VMEM((2, 64, 2048), BF16),
-            pltpu.VMEM((2, 128, 2048), BF16),
+            pltpu.VMEM((512, 512), BF16),
+            pltpu.VMEM((3, 128, 512), BF16),
+            pltpu.VMEM((512, 512), F32),
             pltpu.VMEM((128, 512), BF16),
             pltpu.VMEM((128, 512), BF16),
             pltpu.SemaphoreType.DMA((N_SEMS,)),

time: 122 us -> 98.8 us (0.81); the launches traced: 122 us -> 97.2 us
  Pallas kernels: 120 us -> 95.3 us
    pallas_call x1, Pallas kernels: 120 us -> 95.3 us  [per_device(): pl.pallas_call(kernel, out_shape=jax.ShapeDtypeStruct((8, 2, 32, 512), BF...]
where the time goes in v3:
time: 98.8 us; the launch traced here: 97.2 us
  Pallas kernels  95.3 us (96%)
  local copies, waits for them, and re-layouts  1.88 us (2%)
    pallas_call x1, Pallas kernels, per_device(): pl.pallas_call(kernel, out_shape=jax.ShapeDtypeStruct((8, 2, 32, 512), BF...  95.3 us

profile of v3, /device:TPU:18, one launch (start us, length us, event | category | flops | bytes accessed | tf_op | source)
XLA Modules:
  0.0 97.2 jit_solution(6881412933705421458)
XLA Ops:
  0.0 95.3 %block.1 = bf16[8,2,32,512]{3,2,1,0:T(8,128)(2,1)} custom-call(bf16[128,2048]{1,0:T(8,128)(2,1)} %bitcast.6, s32[8]{0:T(128)} %actions.1, bf16[8,2048]{1,0:T(8,128)(2,1)} %table.1, f32[1,2048]{1,0:T(1,128)} %bitcast.8, bf16[2048,128]{1,0:T(8,128)(2,1)} %wq.1, bf16[16,2048]{1,0:T(8,128)(2,1)} %bitcast.7, f32[2,128]{1,0:T(2,128)} %qk_gain.1, ...), custom_call_target="tpu_custom_call" | custom-call | flops 8522825728 | bytes 14000000 | tf_op jit(solution)/shard_map/block/pallas_call | solution.py:592
  95.3 1.9 %copy.15 = bf16[8,2,32,512]{3,2,1,0:T(8,128)(2,1)} copy(bf16[8,2,32,512]{3,2,1,0:T(8,128)(2,1)} %block.1) | data formatting | bytes 1048576

commit v4 on v3

--- a/solution.py
+++ b/solution.py
@@ -13,8 +13,8 @@
 MASKED = -1e30
 F32 = jnp.float32
 BF16 = jnp.bfloat16
-KINDS = ("q", "kv", "up", "od")
-N_SEMS = 112
+UPS = ("up0", "up1")
+N_SEMS = 128
 TOKENS = 128
 
 
@@ -162,11 +162,12 @@
     weights = {
         "q": Weight(wq, wq_v, True),
         "kv": Weight(wkv, wkv_v, False),
-        "up": Weight(wup, wup_v, True),
+        "up0": Weight(wup.at[:, 0:256], wup_v.at[0], True),
+        "up1": Weight(wup.at[:, 256:512], wup_v.at[1], True),
         "od": Folded(od_v, ods_v),
     }
     fold_copies = [local(wlat, wlat_v), local(wo, wo_v), local(wdown, wdown_v)]
-    own_copy = {kind: local(weights[kind].src, weights[kind].own()) for kind in ("q", "kv", "up")}
+    own_copy = {kind: local(weights[kind].src, weights[kind].own()) for kind in ("q", "kv") + UPS}
     wconv_copy = local(wconv, wconv_v)
 
     pl.semaphore_wait(barrier, 17)
@@ -206,7 +207,7 @@
         for dx in (1, 3, 2):
             arrive(sems[kind, "x", dx], w.piece(core, y, (x + 4 - dx) % 4))
         mine = w.region(core, y)
-        for dy in (1, 3) if kind == "up" else (1, 3, 2):
+        for dy in (1, 3) if kind in UPS else (1, 3, 2):
             sems[kind, "y", dy] = take()
             push(sems[kind, "y", dy], mine, mine, at(dy=dy))
         sems[kind, "c", 0] = take()
@@ -243,12 +244,12 @@
 
     def far_done(kind):
         w = weights[kind]
-        for dy in (0, 1, 3) if kind == "up" else (0, 1, 3, 2):
+        for dy in (0, 1, 3) if kind in UPS else (0, 1, 3, 2):
             arrive(sems[kind, "c", dy], w.region(other, (y + 4 - dy) % 4))
-        for dy, piece in ((1, 0), (3, 1)) if kind == "up" else ():
+        for dy, piece in ((1, 0), (3, 1)) if kind in UPS else ():
             arrive(sems[kind, "c2", dy], w.half_region(other, (y + 2) % 4, piece))
 
-    for kind in ("q", "kv"):
+    for kind in ("q", "kv") + UPS:
         far_start(kind)
     for kind in ("q", "kv"):
         pair_start(kind)
@@ -294,8 +295,7 @@
     od_v[128:640, :] = jnp.dot(wdown_v[...], wlat_v[...], preferred_element_type=F32).astype(BF16)
     token_send("up last", slice(64, 128), slice(192, 256), 1)
     token_send("down first", slice(0, 64), slice(256, 320), 7)
-    for kind in ("up", "od"):
-        far_start(kind)
+    far_start("od")
     for kind in ("q", "kv"):
         row_start(kind)
     ods_v[0] = od_v[...]
@@ -306,22 +306,27 @@
     token_send("down on", slice(320, 384), slice(448, 512), 7)
     for kind in ("q", "kv"):
         column_start(kind)
+    for kind in UPS:
+        row_start(kind)
     for kind in ("q", "kv"):
         pair_share(kind)
-    pair_start("up")
     for kind in ("q", "kv"):
         column_share(kind)
+    for kind in UPS:
+        column_start(kind)
+    for kind in UPS:
+        pair_start(kind)
     token_arrive("up last", slice(192, 256))
     token_arrive("down first", slice(256, 320))
-    row_start("up")
     norm_rows(128, 384)
+    row_start("od")
     pair_start("od")
-    row_start("od")
-    column_start("up")
+    column_relay("up0")
     token_arrive("up on", slice(384, 448))
     token_arrive("down on", slice(448, 512))
     norm_rows(384, 512)
 
+    column_relay("up1")
     for kind in ("q", "kv"):
         own_copy[kind].wait()
         pair_done(kind)
@@ -339,28 +344,30 @@
     kv_columns = (slice(128, 256), slice(256, 384), slice(384, 512), slice(384, 512))
     for slot, (index, (dz, home, away)) in enumerate(zip(kv_sems, routes)):
         push(index, kvt_v.at[:, kv_columns[slot]], kvr_v.at[slot], at(dz=8 - dz))
-    for half in range(2):
+    q_sems = [take() for _ in routes]
+    q_columns = (slice(512, 1024), slice(1024, 1536), slice(1536, 2048), slice(1536, 2048))
+    for half, slots in ((1, (2, 3, 1)), (0, (0,))):
         rows = slice(half * 256, half * 256 + 256)
         q_v[rows, :] = jnp.dot(n_v[rows, :], wq_v[...], preferred_element_type=F32).astype(BF16)
-    q_sems = [take() for _ in routes]
-    q_columns = (slice(512, 1024), slice(1024, 1536), slice(1536, 2048), slice(1536, 2048))
-    for slot, (index, (dz, home, away)) in enumerate(zip(q_sems, routes)):
-        push(index, q_v.at[away], qr_v.at[home, q_columns[slot]], at(dz=8 - dz))
+        for slot in slots:
+            dz, home, away = routes[slot]
+            push(q_sems[slot], q_v.at[away], qr_v.at[home, q_columns[slot]], at(dz=8 - dz))
     qr_v[:, 0:512] = q_v[0:128, :]
 
-    def up_tiles(shard):
-        def tile(index, carry):
-            columns = pl.ds(pl.multiple_of(shard * 512 + index * 256, 256), 256)
-            hidden = jnp.dot(n_v[...], wup_v[:, columns], preferred_element_type=F32)
-            h_v[:, columns] = jax.nn.gelu(hidden, approximate=True).astype(BF16)
-            return carry
-
-        lax.fori_loop(0, 2, tile, 0)
+    def up_tile(chunk, shard):
+        place = chunk * 1024 + shard * 256
+        weight = wup_v[chunk, :, shard * 256 : shard * 256 + 256]
+        for half in range(2):
+            rows = slice(half * 256, half * 256 + 256)
+            hidden = jnp.dot(n_v[rows, :], weight, preferred_element_type=F32)
+            h_v[rows, place : place + 256] = jax.nn.gelu(hidden, approximate=True).astype(BF16)
 
     column_start("od")
-    own_copy["up"].wait()
-    up_tiles(0)
-    pair_share("up")
+    for chunk, kind in enumerate(UPS):
+        own_copy[kind].wait()
+        up_tile(chunk, 0)
+    for kind in UPS:
+        pair_share(kind)
 
     for slot, index in enumerate(kv_sems):
         arrive(index, kvr_v.at[slot])
@@ -440,10 +447,11 @@
     def _():
         share(0).start()
 
-    column_relay("up")
-    pair_done("up")
-    up_tiles(1)
+    for chunk, kind in enumerate(UPS):
+        pair_done(kind)
+        up_tile(chunk, 1)
     column_share("od")
+    column_end("up0")
 
     for index, (slot, (dz, home, away)) in zip(q_sems, enumerate(routes)):
         arrive(index, qr_v.at[home, q_columns[slot]])
@@ -490,30 +498,41 @@
             ao_f[rows, head * 128 : head * 128 + 128] = mixed[head * 8 : head * 8 + 8, :]
         return carry
 
-    lax.fori_loop(0, 16, attend, 0, unroll=2)
-    ao_v[...] = ao_f[...].astype(BF16)
+    at_sems = []
+    sends = (
+        ((1, 0, slice(128, 192)), (7, 1, slice(256, 320)), (2, 2, slice(384, 448))),
+        ((1, 0, slice(192, 256)), (7, 1, slice(320, 384)), (6, 2, slice(448, 512))),
+    )
+    for half in range(2):
+        lax.fori_loop(half * 8, half * 8 + 8, attend, 0, unroll=4)
+        home = slice(half * 64, half * 64 + 64)
+        ao_v[home, :] = ao_f[home, :].astype(BF16)
+        for dz, slot, away in sends[half]:
+            at_sems.append((take(), away))
+            push(at_sems[-1][0], ao_v.at[home, q_columns[slot]], at_v.at[away], at(dz=dz))
     at_v[0:128, :] = ao_v[:, 0:512]
-    at_sems = [take() for _ in routes]
-    for slot, (index, (dz, home, away)) in enumerate(zip(at_sems, routes)):
-        push(index, ao_v.at[home, q_columns[slot]], at_v.at[away], at(dz=dz))
-    column_end("up")
+
+    column_end("up1")
     pair_share("od")
-    far_done("up")
-    up_tiles(2)
-    up_tiles(3)
+    for chunk, kind in enumerate(UPS):
+        far_done(kind)
+        up_tile(chunk, 2)
+        up_tile(chunk, 3)
     pair_done("od")
     far_done("od")
 
     for half in (1, 0):
         rows = slice(half * 256, half * 256 + 256)
         ffn = jnp.zeros((256, 512), F32)
-        for shard in range(4):
+        for place in range(8):
+            chunk, shard = place // 4, place % 4
             ffn += jnp.dot(
-                h_v[rows, shard * 512 : shard * 512 + 512], ods_v[shard, 128:640, :],
+                h_v[rows, place * 256 : place * 256 + 256],
+                ods_v[shard, 128 + chunk * 256 : 384 + chunk * 256, :],
                 preferred_element_type=F32,
             )
         ffn_f[rows, :] = ffn
-    for index, (dz, home, away) in zip(at_sems, routes):
+    for index, away in at_sems:
         arrive(index, at_v.at[away])
     sum_sems = [take() for _ in routes]
     places = ((0, slice(0, 128)), (1, slice(0, 128)), (2, slice(0, 64)), (2, slice(64, 128)))
@@ -601,7 +620,7 @@
             pltpu.VMEM((128, 2048), BF16),
             pltpu.VMEM((2048, 512), BF16),
             pltpu.VMEM((64, 2048), BF16),
-            pltpu.VMEM((2048, 2048), BF16),
+            pltpu.VMEM((2, 2048, 1024), BF16),
             pltpu.VMEM((128, 2048), BF16),
             pltpu.VMEM((512, 2048), BF16),
             pltpu.VMEM((2048, 512), BF16),
@@ -629,7 +648,7 @@
             pltpu.VMEM((128, 512), BF16),
             pltpu.SemaphoreType.DMA((N_SEMS,)),
             pltpu.SemaphoreType.DMA((N_SEMS,)),
-            pltpu.SemaphoreType.DMA((8,)),
+            pltpu.SemaphoreType.DMA((9,)),
         ],
         compiler_params=pltpu.CompilerParams(
             collective_id=1, has_side_effects=True, vmem_limit_bytes=60 * 1024 * 1024

time: 98.8 us -> 93.6 us (0.947); the launches traced: 97.2 us -> 93.4 us
  Pallas kernels: 95.3 us -> 91.5 us
    pallas_call x1, Pallas kernels: 95.3 us -> 91.5 us  [per_device(): pl.pallas_call(kernel, out_shape=jax.ShapeDtypeStruct((8, 2, 32, 512), BF...]
where the time goes in v4:
time: 93.6 us; the launch traced here: 93.4 us
  Pallas kernels  91.5 us (98%)
  local copies, waits for them, and re-layouts  1.88 us (2%)
    pallas_call x1, Pallas kernels, per_device(): pl.pallas_call(kernel, out_shape=jax.ShapeDtypeStruct((8, 2, 32, 512), BF...  91.5 us
    unnamed x1, local copies, waits for them, and re-layouts  1.88 us

profile of v4, /device:TPU:18, one launch (start us, length us, event | category | flops | bytes accessed | tf_op | source)
XLA Modules:
  0.0 93.4 jit_solution(8904517730836211254)
XLA Ops:
  0.0 91.5 %block.1 = bf16[8,2,32,512]{3,2,1,0:T(8,128)(2,1)} custom-call(bf16[128,2048]{1,0:T(8,128)(2,1)} %bitcast.6, s32[8]{0:T(128)} %actions.1, bf16[8,2048]{1,0:T(8,128)(2,1)} %table.1, f32[1,2048]{1,0:T(1,128)} %bitcast.8, bf16[2048,128]{1,0:T(8,128)(2,1)} %wq.1, bf16[16,2048]{1,0:T(8,128)(2,1)} %bitcast.7, f32[2,128]{1,0:T(2,128)} %qk_gain.1, ...), custom_call_target="tpu_custom_call" | custom-call | flops 8522825728 | bytes 14000000 | tf_op jit(solution)/shard_map/block/pallas_call | solution.py:611
  91.5 1.9 %copy.15 = bf16[8,2,32,512]{3,2,1,0:T(8,128)(2,1)} copy(bf16[8,2,32,512]{3,2,1,0:T(8,128)(2,1)} %block.1) | data formatting | bytes 1048576

commit v5 on v4

--- a/solution.py
+++ b/solution.py
@@ -514,24 +514,32 @@
 
     column_end("up1")
     pair_share("od")
-    for chunk, kind in enumerate(UPS):
-        far_done(kind)
-        up_tile(chunk, 2)
-        up_tile(chunk, 3)
+    far_done("up0")
+    up_tile(0, 2)
+    up_tile(0, 3)
     pair_done("od")
     far_done("od")
 
-    for half in (1, 0):
-        rows = slice(half * 256, half * 256 + 256)
-        ffn = jnp.zeros((256, 512), F32)
-        for place in range(8):
+    def second_layer(rows, blocks):
+        total = jnp.zeros((256, 512), F32)
+        for place in blocks:
             chunk, shard = place // 4, place % 4
-            ffn += jnp.dot(
+            total += jnp.dot(
                 h_v[rows, place * 256 : place * 256 + 256],
                 ods_v[shard, 128 + chunk * 256 : 384 + chunk * 256, :],
                 preferred_element_type=F32,
             )
-        ffn_f[rows, :] = ffn
+        return total
+
+    for half in (1, 0):
+        rows = slice(half * 256, half * 256 + 256)
+        ffn_f[rows, :] = second_layer(rows, range(6))
+    far_done("up1")
+    up_tile(1, 2)
+    up_tile(1, 3)
+    for half in (1, 0):
+        rows = slice(half * 256, half * 256 + 256)
+        ffn_f[rows, :] += second_layer(rows, (6, 7))
     for index, away in at_sems:
         arrive(index, at_v.at[away])
     sum_sems = [take() for _ in routes]

time: 93.6 us -> 93.6 us (level)
  no operation moved by 1% of the time
where the time goes in v5:
time: 93.6 us; the launch traced here: 93.4 us
  Pallas kernels  91.5 us (98%)
  local copies, waits for them, and re-layouts  1.88 us (2%)
    pallas_call x1, Pallas kernels, per_device(): pl.pallas_call(kernel, out_shape=jax.ShapeDtypeStruct((8, 2, 32, 512), BF...  91.5 us
    unnamed x1, local copies, waits for them, and re-layouts  1.88 us

profile of v5, /device:TPU:18, one launch (start us, length us, event | category | flops | bytes accessed | tf_op | source)
XLA Modules:
  0.0 93.4 jit_solution(6063505450681011477)
XLA Ops:
  0.0 91.5 %block.1 = bf16[8,2,32,512]{3,2,1,0:T(8,128)(2,1)} custom-call(bf16[128,2048]{1,0:T(8,128)(2,1)} %bitcast.6, s32[8]{0:T(128)} %actions.1, bf16[8,2048]{1,0:T(8,128)(2,1)} %table.1, f32[1,2048]{1,0:T(1,128)} %bitcast.8, bf16[2048,128]{1,0:T(8,128)(2,1)} %wq.1, bf16[16,2048]{1,0:T(8,128)(2,1)} %bitcast.7, f32[2,128]{1,0:T(2,128)} %qk_gain.1, ...), custom_call_target="tpu_custom_call" | custom-call | flops 8522825728 | bytes 14000000 | tf_op jit(solution)/shard_map/block/pallas_call | solution.py:619
  91.5 1.9 %copy.15 = bf16[8,2,32,512]{3,2,1,0:T(8,128)(2,1)} copy(bf16[8,2,32,512]{3,2,1,0:T(8,128)(2,1)} %block.1) | data formatting | bytes 1048576
